TPU v7x, 128 devices: a whole 4x4x4 slice. The times are simulated.
128 devices in a mesh: replica: 16 (over x, z_lo, core), tensor: 8 (over z_hi, y).
Axes of the slice: x: 4, y: 4, z: 4 (z_hi: 2, z_lo: 2; z = z_hi * 2 + z_lo), core: 2. Of those that a mesh axis runs over, the one named last changes fastest.
Arguments:
- hidden: bfloat16 [4, 128, 8192], P(None, 'replica'), may hold values from -6 to 6
- query_weight: bfloat16 [8192, 4096], P(None, 'tensor'), may hold values from -0.0625 to 0.0625
- keyval_weight: bfloat16 [2, 8192, 1024], P(None, None, 'tensor'), may hold values from -0.0625 to 0.0625
- output_weight: bfloat16 [4096, 8192], P('tensor'), may hold values from -0.09375 to 0.09375
- adapter_down_stack: bfloat16 [3, 8192, 64], P(None, 'replica'), may hold values from -0.0625 to 0.0625
- adapter_query_up: bfloat16 [64, 4096], P(None, 'replica'), may hold values from -0.75 to 0.75
- adapter_keyval_up: bfloat16 [2, 64, 1024], P(None, None, 'replica'), may hold values from -0.75 to 0.75
- adapter_output_down: bfloat16 [4096, 64], P('replica'), may hold values from -0.09375 to 0.09375
- adapter_output_up: bfloat16 [64, 8192], P(None, 'replica'), may hold values from -0.75 to 0.75
- owner: int32 [16], replicated, may hold values from 0 to 15, each once
- key_cache_rows: bfloat16 [128, 1024, 1024], P('replica', None, 'tensor'), may hold values from -150 to 150
- value_cache_rows: bfloat16 [128, 1024, 1024], P('replica', None, 'tensor'), may hold values from -6 to 6
- lengths: int32 [128], P('replica'), may hold values from 1 to 1024, 81920 in all
Outputs:
- block_out: bfloat16 [4, 128, 8192], P(None, 'replica', 'tensor')
All inputs are finite; a program needn't handle non-finite values. No bound on the sum of `lengths` on one device may be relied on, other than what follows from the above.
Results may differ from a plain program's by a relative error of at most 0.018.
Values may be sent and summed in bfloat16 or wider, within the bound.
A program may use at most 128 MiB of HBM per device.

v0:
```python
import math

import jax
import jax.numpy as jnp
from jax import lax
from jax.sharding import PartitionSpec as P

HEAD_DIM = 128


adapter_scale = 0.5
masked_score = -1e30


def recover_weight(stored, owner, reduce_axis):
    count = owner.shape[0]
    block_size = stored.shape[reduce_axis] // count
    block_shape = stored.shape[:reduce_axis] + (count, block_size) + stored.shape[reduce_axis + 1 :]
    blocks = jnp.take(stored.reshape(block_shape), owner, axis=reduce_axis)
    return blocks.reshape(stored.shape)


def combine_block(frozen_weight, down_factor, up_factor):
    rank_update = jnp.dot(down_factor, up_factor, preferred_element_type=jnp.float32)
    return (frozen_weight.astype(jnp.float32) + adapter_scale * rank_update).astype(jnp.bfloat16)


def attend(
    hidden, merged_query, merged_keyval, merged_out, key_cache_rows, value_cache_rows, lengths
):
    steps, batch, width = hidden.shape
    inputs = hidden.reshape(steps * batch, width)
    kv_heads = key_cache_rows.shape[2] // HEAD_DIM
    group = merged_query.shape[1] // (kv_heads * HEAD_DIM)
    queries = jnp.dot(inputs, merged_query, preferred_element_type=jnp.float32).astype(jnp.bfloat16)
    queries = queries.reshape(steps, batch, kv_heads, group, HEAD_DIM)
    fresh = jnp.einsum(
        "nd,cde->cne", inputs, merged_keyval, preferred_element_type=jnp.float32
    ).astype(jnp.bfloat16)
    fresh = fresh.reshape(2, steps, batch, kv_heads, HEAD_DIM)
    new_keys = fresh[0]
    new_values = fresh[1]
    inv_scale = 1.0 / math.sqrt(HEAD_DIM)
    past_keys = key_cache_rows.reshape(batch, -1, kv_heads, HEAD_DIM)
    past_values = value_cache_rows.reshape(batch, -1, kv_heads, HEAD_DIM)
    slots = past_keys.shape[1]
    past_scores = (
        jnp.einsum("srkgd,rlkd->srkgl", queries, past_keys, preferred_element_type=jnp.float32)
        * inv_scale
    )
    visible = jnp.arange(slots, dtype=jnp.int32)[None, :] < lengths[:, None]
    past_scores = jnp.where(visible[None, :, None, None, :], past_scores, masked_score)
    new_scores = (
        jnp.einsum("srkgd,trkd->srkgt", queries, new_keys, preferred_element_type=jnp.float32)
        * inv_scale
    )
    causal = (
        jnp.arange(steps, dtype=jnp.int32)[None, :] <= jnp.arange(steps, dtype=jnp.int32)[:, None]
    )
    new_scores = jnp.where(causal[:, None, None, None, :], new_scores, masked_score)
    highest = jnp.maximum(
        jnp.max(past_scores, -1, keepdims=True), jnp.max(new_scores, -1, keepdims=True)
    )
    past_exp = jnp.exp(past_scores - highest)
    new_exp = jnp.exp(new_scores - highest)
    denominator = jnp.sum(past_exp, -1, keepdims=True) + jnp.sum(new_exp, -1, keepdims=True)
    past_weights = (past_exp / denominator).astype(jnp.bfloat16)
    new_weights = (new_exp / denominator).astype(jnp.bfloat16)
    context = jnp.einsum(
        "srkgl,rlkd->srkgd", past_weights, past_values, preferred_element_type=jnp.float32
    )
    context = context + jnp.einsum(
        "srkgt,trkd->srkgd", new_weights, new_values, preferred_element_type=jnp.float32
    )
    context = context.astype(jnp.bfloat16).reshape(steps * batch, -1)
    partial_sums = jnp.dot(context, merged_out, preferred_element_type=jnp.float32)
    return partial_sums.reshape(steps, batch, width)


def body(
    hidden,
    query_weight,
    keyval_weight,
    output_weight,
    adapter_down_stack,
    adapter_query_up,
    adapter_keyval_up,
    adapter_output_down,
    adapter_output_up,
    owner,
    key_cache_rows,
    value_cache_rows,
    lengths,
):
    tensor_index = lax.axis_index("tensor")
    replica_index = lax.axis_index("replica")
    query_cols = query_weight.shape[1]
    keyval_cols = keyval_weight.shape[2]
    query_up_factor, keyval_up_factor, output_down_factor = (
        lax.all_gather(adapter_query_up, "replica", axis=1, tiled=True),
        lax.all_gather(adapter_keyval_up, "replica", axis=2, tiled=True),
        lax.all_gather(adapter_output_down, "replica", axis=0, tiled=True),
    )
    query_up_factor = lax.dynamic_slice_in_dim(
        recover_weight(query_up_factor, owner, 1), tensor_index * query_cols, query_cols, 1
    )
    keyval_up_factor = lax.dynamic_slice_in_dim(
        recover_weight(keyval_up_factor, owner, 2), tensor_index * keyval_cols, keyval_cols, 2
    )
    output_down_factor = lax.dynamic_slice_in_dim(
        recover_weight(output_down_factor, owner, 0), tensor_index * query_cols, query_cols, 0
    )
    section_index = jnp.sum(
        jnp.where(owner == replica_index, jnp.arange(owner.shape[0], dtype=jnp.int32), 0)
    )
    row_total = adapter_down_stack.shape[1]
    query_rows = combine_block(
        lax.dynamic_slice_in_dim(query_weight, section_index * row_total, row_total, 0),
        adapter_down_stack[0],
        query_up_factor,
    )
    frozen_keyval_weight = lax.dynamic_slice_in_dim(
        keyval_weight, section_index * row_total, row_total, 1
    )
    keyval_rows = jnp.stack(
        [
            combine_block(frozen_keyval_weight[0], adapter_down_stack[1], keyval_up_factor[0]),
            combine_block(frozen_keyval_weight[1], adapter_down_stack[2], keyval_up_factor[1]),
        ]
    )
    merged_query, merged_keyval = (
        lax.all_gather(query_rows, "replica", axis=0, tiled=True),
        lax.all_gather(keyval_rows, "replica", axis=1, tiled=True),
    )
    merged_query = recover_weight(merged_query, owner, 0)
    merged_keyval = recover_weight(merged_keyval, owner, 1)
    column_total = adapter_output_up.shape[1]
    out_cols = combine_block(
        lax.dynamic_slice_in_dim(output_weight, section_index * column_total, column_total, 1),
        output_down_factor,
        adapter_output_up,
    )
    merged_out = recover_weight(lax.all_gather(out_cols, "replica", axis=1, tiled=True), owner, 1)
    partial_sums = attend(
        hidden, merged_query, merged_keyval, merged_out, key_cache_rows, value_cache_rows, lengths
    )
    results = []
    for position in range(partial_sums.shape[0]):
        results.append(
            lax.psum_scatter(
                partial_sums[position].astype(jnp.bfloat16),
                "tensor",
                scatter_dimension=1,
                tiled=True,
            ).astype(jnp.float32)
        )
    summed = jnp.stack(results)
    return summed.astype(jnp.bfloat16)


def solution(mesh):
    in_specs = (
        P(None, "replica", None),
        P(None, "tensor"),
        P(None, None, "tensor"),
        P("tensor", None),
        P(None, "replica", None),
        P(None, "replica"),
        P(None, None, "replica"),
        P("replica", None),
        P(None, "replica"),
        P(),
        P("replica", None, "tensor"),
        P("replica", None, "tensor"),
        P("replica"),
    )
    out_specs = P(None, "replica", "tensor")
    return jax.shard_map(body, mesh=mesh, in_specs=in_specs, out_specs=out_specs, check_vma=False)
```

profile of v0, /device:TPU:1, one launch (start us, length us, event | category | flops | bytes accessed | tf_op | source)
XLA Modules:
  0.0 531.0 jit_solution(14805058041033121584)
XLA Ops:
  6.6 0.8 compare_and_fusion
  7.4 1.3 compare_select_fusion
  9.5 0.8 copy.59
  10.3 22.9 %all_gather.20 = bf16[2,64,1024]{1,0,2:T(2,128)(2,1)S(1)} all-gather(bf16[2,64,64]{1,0,2:T(2,128)(2,1)S(1)} %copy.59), channel_id=1, replica_groups=mesh['replica'=16,'tensor'=8] {'replica'}, dimensions={2}, use_global_device_ids=true | all-gather | bytes 278528 | tf_op jit(solution)/shard_map/all_gather | solution.py:101
  33.3 0.5 copy.61
  33.7 0.6 gather_fusion.2
  34.4 0.3 copy.62
  34.8 0.3 gather.34
  35.1 1.0 constant_dynamic-slice_fusion
  36.5 1.1 fusion.21
  37.5 1.1 fusion.22
  38.6 0.7 pad_maximum_fusion
  39.5 1.1 constant_dynamic-slice_fusion.2
  40.8 17.9 %all_gather.18 = bf16[64,4096]{1,0:T(8,128)(2,1)S(1)} all-gather(bf16[64,256]{1,0:T(8,128)(2,1)S(1)} %copy-done.3), channel_id=1, replica_groups=mesh['replica'=16,'tensor'=8] {'replica'}, dimensions={1}, use_global_device_ids=true | all-gather | bytes 557056 | tf_op jit(solution)/shard_map/all_gather | solution.py:100
  58.8 1.4 gather_fusion
  60.1 1.1 copy.94
  61.3 2.0 fusion.7
  63.4 20.4 %all_gather.22 = bf16[4096,64]{0,1:T(8,128)(2,1)S(1)} all-gather(bf16[256,64]{0,1:T(8,128)(2,1)S(1)} %copy-done.4), channel_id=1, replica_groups=mesh['replica'=16,'tensor'=8] {'replica'}, dimensions={0}, use_global_device_ids=true | all-gather | bytes 557056 | tf_op jit(solution)/shard_map/all_gather | solution.py:102
  83.8 0.6 gather_fusion.4
  84.5 2.2 fusion.8
  87.1 6.4 %copy.82 = bf16[2,8192,128]{2,1,0:T(8,128)(2,1)} copy(bf16[2,8192,128]{1,2,0:T(8,128)(2,1)} %all-gather.6.cloned.1.call-done) | data formatting | bytes 8388608 | tf_op jit(solution)/shard_map/reshape | solution.py:19
  93.5 5.3 gather_fusion.3
  98.8 2.8 select_bitcast_fusion.1
  101.6 0.4 copy.64
  102.1 0.8 fusion.36
  102.9 30.2 %all-gather.4.cloned.1.call-done = bf16[8192,512]{0,1:T(8,128)(2,1)} async-done(((bf16[512,512]{0,1:T(8,128)(2,1)}), bf16[8192,512]{0,1:T(8,128)(2,1)}) %all-gather.4.cloned.1.call-update) | async-done | bytes 8388624 | tf_op jit(solution)/shard_map/all_gather | solution.py:132
  133.1 12.0 %copy.79 = bf16[8192,512]{1,0:T(8,128)(2,1)} copy(bf16[8192,512]{0,1:T(8,128)(2,1)} %all-gather.4.cloned.1.call-done) | data formatting | bytes 16777216 | tf_op jit(solution)/shard_map/reshape | solution.py:19
  145.1 8.2 %gather_fusion.1 = bf16[16,512,512]{2,1,0:T(8,128)(2,1)} fusion(bf16[16,512,512]{2,1,0:T(8,128)(2,1)} %bitcast.162, s32[1024]{0:T(1024)S(1)} %pad_clamp_fusion), kind=kCustom, calls=%fused_computation.1 | custom fusion | bytes 16777280 | tf_op jit(solution)/shard_map/jit(_take)/gather | solution.py:19
  153.3 34.5 %all-gather.8.cloned.1.call-done = bf16[512,8192]{1,0:T(8,128)(2,1)} async-done(((bf16[512,512]{1,0:T(8,128)(2,1)}), bf16[512,8192]{1,0:T(8,128)(2,1)}) %all-gather.8.cloned.1.call-update) | async-done | bytes 8388624 | tf_op jit(solution)/shard_map/all_gather | solution.py:143
  187.8 7.5 %copy.117 = bf16[64,16,8,512]{3,2,0,1:T(8,128)(2,1)} copy(bf16[64,16,8,512]{3,2,1,0:T(8,128)(2,1)} %bitcast.165) | data formatting | bytes 16777216 | tf_op jit(solution)/shard_map/reshape | solution.py:19
  195.3 8.2 %gather_fusion.5 = bf16[16,512,512]{2,1,0:T(8,128)(2,1)} fusion(bf16[512,16,512]{2,0,1:T(8,128)(2,1)} %bitcast.161, s32[1024]{0:T(1024)S(1)} %pad_clamp_fusion), kind=kCustom, calls=%fused_computation.5 | custom fusion | bytes 16777280 | tf_op jit(solution)/shard_map/jit(_take)/gather | solution.py:19
  203.5 9.4 %broadcast_select_fusion = (bf16[16,512,512]{2,1,0:T(8,128)(2,1)S(1)}, bf16[512,16,512]{2,0,1:T(8,128)(2,1)}) fusion(bf16[16,512,512]{2,1,0:T(8,128)(2,1)} %gather_fusion.1, pred[16]{0:T(512)(128)(4,1)S(1)} %compare_and_fusion, bf16[16,512,512]{2,1,0:T(8,128)(2,1)} %gather_fusion.5), kind=kLoop, calls=%fused_computation.9 | loop fusion | flops 8388608 | bytes 33554448 | tf_op jit(solution)/shard_map/jit(_take)/select_n | solution.py:19
  212.9 1.5 fusion.28
  214.4 0.4 fusion.69
  214.8 0.8 fusion.68
  215.7 0.3 fusion.40
  216.0 12.3 %copy.73 = bf16[512,16,512]{0,2,1:T(8,128)(2,1)} copy(bf16[512,16,512]{2,0,1:T(8,128)(2,1)} %get-tuple-element.14) | data formatting | bytes 16777216 | tf_op jit(solution)/shard_map/jit(_take)/select_n | solution.py:19
  228.4 2.1 fusion.24
  230.7 5.9 %convolution_convert_fusion = bf16[32,8192]{1,0:T(8,128)(2,1)S(1)} fusion(bf16[512,8192]{0,1:T(8,128)(2,1)} %bitcast.160, bf16[4,8,1,4,128]{4,3,0,1,2:T(4,128)(2,1)S(1)} %fusion.29), kind=kOutput, calls=%fused_computation.6 | convolution fusion | flops 268697600 | bytes 8945664 | tf_op jit(solution)/shard_map/dot_general | solution.py:76
  236.6 0.8 fusion.67
  237.5 0.5 reduce-scatter.7.cloned.1.call-update
  238.1 0.5 reduce-scatter.9.cloned.1.call-update
  238.7 0.7 reduce-scatter.11.cloned.1.call-update
  239.4 66.6 %reduce-scatter.5.cloned.1.call-done = bf16[8,1024]{1,0:T(8,128)(2,1)} async-done(((bf16[8,8192]{1,0:T(8,128)(2,1)}), bf16[8,1024]{1,0:T(8,128)(2,1)}) %reduce-scatter.5.cloned.1.call-update) | async-done | bytes 16400 | tf_op jit(solution)/shard_map/reduce_scatter | solution.py:150
  306.0 72.2 %reduce-scatter.7.cloned.1.call-done = bf16[8,1024]{1,0:T(8,128)(2,1)} async-done(((bf16[8,8192]{1,0:T(8,128)(2,1)}), bf16[8,1024]{1,0:T(8,128)(2,1)}) %reduce-scatter.7.cloned.1.call-update) | async-done | bytes 16400 | tf_op jit(solution)/shard_map/reduce_scatter | solution.py:150
  378.2 72.2 %reduce-scatter.9.cloned.1.call-done = bf16[8,1024]{1,0:T(8,128)(2,1)} async-done(((bf16[8,8192]{1,0:T(8,128)(2,1)}), bf16[8,1024]{1,0:T(8,128)(2,1)}) %reduce-scatter.9.cloned.1.call-update) | async-done | bytes 16400 | tf_op jit(solution)/shard_map/reduce_scatter | solution.py:150
  450.4 72.4 %reduce-scatter.11.cloned.1.call-done = bf16[8,1024]{1,0:T(8,128)(2,1)} async-done(((bf16[8,8192]{1,0:T(8,128)(2,1)}), bf16[8,1024]{1,0:T(8,128)(2,1)}) %reduce-scatter.11.cloned.1.call-update) | async-done | bytes 16400 | tf_op jit(solution)/shard_map/reduce_scatter | solution.py:150
  522.8 1.4 pad_maximum_fusion.1
  (45 shorter events, 1.9 us)
Async XLA Ops:
  6.5 208.3 %copy-start = (bf16[8,1024,128]{2,1,0:T(8,128)(2,1)S(1)}, bf16[8,1024,128]{2,1,0:T(8,128)(2,1)}, u32[]{:S(2)}) copy-start(bf16[8,1024,128]{2,1,0:T(8,128)(2,1)} %param.23) | copy-start | bytes 6291460
  6.5 34.3 %copy-start.3 = (bf16[64,256]{1,0:T(8,128)(2,1)S(1)}, bf16[64,256]{1,0:T(8,128)(2,1)}, u32[]{:S(2)}) copy-start(bf16[64,256]{1,0:T(8,128)(2,1)} %param.18) | copy-start | bytes 98308
  6.5 56.8 %copy-start.4 = (bf16[256,64]{0,1:T(8,128)(2,1)S(1)}, bf16[256,64]{0,1:T(8,128)(2,1)}, u32[]{:S(2)}) copy-start(bf16[256,64]{0,1:T(8,128)(2,1)} %param.20) | copy-start | bytes 98308
  6.5 80.5 %all-gather.6.cloned.1.call-start = ((), (), s32[]{:S(2)}) async-start(), calls=%async_computation.5 | async-start | bytes 4456448 | tf_op jit(solution)/shard_map/all_gather | solution.py:133
  34.4 50.1 %copy-start.2 = (bf16[64,512]{1,0:T(8,128)(2,1)S(1)}, bf16[64,512]{1,0:T(8,128)(2,1)}, u32[]{:S(2)}) copy-start(bf16[64,512]{1,0:T(8,128)(2,1)} %param.21) | copy-start | bytes 196612
  35.1 51.9 %copy-start.5 = (s32[8]{0:T(128)S(1)}, s32[8]{0:T(128)}, u32[]{:S(2)}) copy-start(s32[8]{0:T(128)} %param.25) | copy-start | bytes 100
  39.3 93.8 %all-gather.4.cloned.1.call-start = ((), (), s32[]{:S(2)}) async-start(), calls=%async_computation.4 | async-start | bytes 8912896 | tf_op jit(solution)/shard_map/all_gather | solution.py:132
  63.3 124.5 %all-gather.8.cloned.1.call-start = ((), (), s32[]{:S(2)}) async-start(), calls=%async_computation.6 | async-start | bytes 8912896 | tf_op jit(solution)/shard_map/all_gather | solution.py:143
  86.7 219.2 %reduce-scatter.5.cloned.1.call-start = ((), (), s32[]{:S(2)}) async-start(), calls=%async_computation.7 | async-start | bytes 147456 | tf_op jit(solution)/shard_map/reduce_scatter | solution.py:150
  98.8 3.3 copy-start.1
  237.5 140.7 %reduce-scatter.7.cloned.1.call-start = ((), (), s32[]{:S(2)}) async-start(), calls=%async_computation.8 | async-start | bytes 147456 | tf_op jit(solution)/shard_map/reduce_scatter | solution.py:150
  238.1 212.4 %reduce-scatter.9.cloned.1.call-start = ((), (), s32[]{:S(2)}) async-start(), calls=%async_computation.9 | async-start | bytes 147456 | tf_op jit(solution)/shard_map/reduce_scatter | solution.py:150
  238.6 284.2 %reduce-scatter.11.cloned.1.call-start = ((), (), s32[]{:S(2)}) async-start(), calls=%async_computation.10 | async-start | bytes 147456 | tf_op jit(solution)/shard_map/reduce_scatter | solution.py:150
Sparse Core Ops, SparseCore 0:
  39.5 39.5 all-gather.5
  80.7 52.4 all-gather.3
  134.8 52.9 all-gather.7
  237.6 68.3 reduce-scatter.4
  309.4 68.7 reduce-scatter.6
  381.6 68.7 reduce-scatter.8
  454.0 68.7 reduce-scatter.10
where the time goes:
time: 534 us; the launch traced here: 531 us
  waiting for transfers between devices  350 us (66%)
  local copies, waits for them, and re-layouts  70 us (13%)
  blocking collectives  61.3 us (11%)
  matrix products  18.1 us (3%)
  other arithmetic  16.9 us (3%)
  between operations  14.4 us (3%)
    reduce_scatter x4, waiting for transfers between devices, body(): lax.psum_scatter(partial_sums[position].astype(jnp.bfloat16), 'tensor', s...  283 us
    all_gather x1, waiting for transfers between devices, body(): lax.all_gather(out_cols, 'replica', axis=1, tiled=True)  34.5 us
    all_gather x1, waiting for transfers between devices, body(): lax.all_gather(query_rows, 'replica', axis=0, tiled=True)  30.2 us
    reshape x6, local copies, waits for them, and re-layouts, recover_weight(): blocks = jnp.take(stored.reshape(block_shape), owner, axis=reduce_axis)  26.5 us
    gather x10, local copies, waits for them, and re-layouts, recover_weight(): blocks = jnp.take(stored.reshape(block_shape), owner, axis=reduce_axis)  26.1 us
    all_gather x1, blocking collectives, body(): lax.all_gather(adapter_keyval_up, 'replica', axis=2, tiled=True)  22.9 us
    all_gather x1, blocking collectives, body(): lax.all_gather(adapter_output_down, 'replica', axis=0, tiled=True)  20.4 us
    all_gather x1, blocking collectives, body(): lax.all_gather(adapter_query_up, 'replica', axis=1, tiled=True)  17.9 us
  transfers between devices with their start and end apart: 7, of which 6 were waited for; matrix products, arithmetic and copies ran while one was open for 8% of the time, Pallas kernels for 0%

commit v1 on v0

v1 whole, which is shorter than its diff:
```python
import math

import jax
import jax.numpy as jnp
from jax import lax
from jax.experimental import pallas as pl
from jax.experimental.pallas import tpu as pltpu
from jax.sharding import PartitionSpec as P

MESH = pl.DeviceIdType.MESH
BF16 = jnp.bfloat16
F32 = jnp.float32
HEAD_DIM = 128
SCALE = 0.5
MASKED = -1e30
R, T = 16, 8
K_PARTS = 4


def kernel(
    owner, lengths, hid, wq, wkv, wo, dstk, qup, kvup, odn, oup, kc, vc,
    out_ref,
    hid_v, wq_v, wkv_v, wo_v, k_v, v_v, d_v, qup_v, kvup_v, odn_v, oup_v, upk, odp,
    p1s, p1r, p1os, p1or, hc, hcs, dc, p2s, p2r, p2os, p2or,
    uqk, uv, q_s, kn_s, vn_s, acc_q, acc_kv, ctx_s, cx, do_v, uo_v, rss, rsr,
    small_sem, q_sem, kv_sem, cache_sem, wo_sem, hc_sem,
    p1_ss, p1_rs, p1o_ss, p1o_rs, p2_ss, p2_rs, p2o_ss, p2o_rs, rs_ss, rs_rs,
):
    r, t = lax.axis_index("replica"), lax.axis_index("tensor")
    x, zl, c = r // 4, lax.rem(r // 2, 2), lax.rem(r, 2)
    other = r + 1 - 2 * c
    mine = t * 2 + c
    rows = 8192 // K_PARTS

    t64 = pl.multiple_of(t * 64, 64)
    small = [
        pltpu.make_async_copy(dstk.at[:, pl.ds(t64, 64), :], d_v, small_sem.at[0]),
        pltpu.make_async_copy(qup, qup_v, small_sem.at[1]),
        pltpu.make_async_copy(kvup, kvup_v, small_sem.at[2]),
        pltpu.make_async_copy(odn, odn_v, small_sem.at[3]),
        pltpu.make_async_copy(oup, oup_v, small_sem.at[4]),
    ]
    hid_copy = pltpu.make_async_copy(hid, hid_v, small_sem.at[5])
    for copy in small:
        copy.start()
    hid_copy.start()

    def q_copies(i):
        at = pl.ds(pl.multiple_of(i * rows, rows), rows)
        return [
            pltpu.make_async_copy(wq.at[at, :], wq_v.at[at, :], q_sem.at[i]),
            pltpu.make_async_copy(wkv.at[0, at, :], wkv_v.at[at, pl.ds(0, 128)], kv_sem.at[0, i]),
            pltpu.make_async_copy(wkv.at[1, at, :], wkv_v.at[at, pl.ds(128, 128)], kv_sem.at[1, i]),
        ]

    for i in range(K_PARTS):
        for copy in q_copies(i):
            copy.start()
    cache = [
        pltpu.make_async_copy(kc, k_v.at[:, pl.ds(0, 1024), :], cache_sem.at[0]),
        pltpu.make_async_copy(vc, v_v.at[:, pl.ds(0, 1024), :], cache_sem.at[1]),
    ]
    for copy in cache:
        copy.start()
    heads = [lax.rem(t + i, T) for i in (6, 2, 5, 3, 4, 7, 1, 0)]
    wo_copies = [
        pltpu.make_async_copy(
            wo.at[:, pl.ds(pl.multiple_of(heads[i] * 1024, 1024), 1024)], wo_v.at[i], wo_sem.at[i]
        )
        for i in range(T)
    ]
    for copy in wo_copies:
        copy.start()

    barrier = pltpu.get_barrier_semaphore()
    ring = [
        (lax.rem(x + dx, 4) * 4 + (zl if dz == 0 else 1 - zl) * 2 + (c if dc_ == 0 else 1 - c), t)
        for dx, dz in ((2, 1), (2, 0), (1, 1), (3, 1), (1, 0), (3, 0), (0, 1), (0, 0))
        for dc_ in (0, 1)
        if dx or dz or dc_
    ]
    cross = [
        (r if dc_ == 0 else other, lax.rem(t + i, T))
        for i in (6, 2, 5, 3, 4, 7, 1, 0)
        for dc_ in (0, 1)
        if i or dc_
    ]
    greeted = ring + [(rr, tt) for j, (rr, tt) in enumerate(cross) if j < 14]
    for peer in greeted:
        pl.semaphore_signal(barrier, inc=1, device_id=peer, device_id_type=MESH)

    for copy in small:
        copy.wait()
    lane = lax.broadcasted_iota(jnp.int32, (16, 128), 1)
    upk[0] = qup_v[:, 0:128]
    upk[1] = qup_v[:, 128:256]
    upk[2] = jnp.concatenate([kvup_v[0], kvup_v[1]], axis=1)
    upk[3] = jnp.zeros((64, 128), BF16)
    odp[...] = jnp.concatenate([odn_v[0:128, :], odn_v[128:256, :]], axis=1)
    t32 = pl.multiple_of(lax.rem(t, 2) * 32, 32)
    u_rows = upk[t // 2, pl.ds(t32, 32), :]
    uo_rows = oup_v[pl.ds(t32, 32), pl.ds(pl.multiple_of((t // 2) * 128, 128), 128)]
    do_rows = odp[pl.ds(pl.multiple_of(lax.rem(t, 4) * 32, 32), 32), :]
    for j in range(2):
        p1s[j, 0:32, :] = jnp.concatenate(
            [d_v[0, j * 32 : j * 32 + 32, :], d_v[1, j * 32 : j * 32 + 32, :]], axis=1
        )
        p1s[j, 32:48, :] = jnp.concatenate(
            [d_v[2, j * 32 : j * 32 + 16, :], d_v[2, j * 32 + 16 : j * 32 + 32, :]], axis=1
        )
        p1s[j, 48:64, :] = u_rows[j * 16 : j * 16 + 16]
        p1os[j, 0:16, :] = uo_rows[j * 16 : j * 16 + 16]
        p1os[j, 16:32, :] = do_rows[j * 16 : j * 16 + 16]

    pl.semaphore_wait(barrier, len(greeted))

    sends = []

    def send(src, dst, ss, rs, peer):
        copy = pltpu.make_async_remote_copy(
            src_ref=src, dst_ref=dst, send_sem=ss, recv_sem=rs, device_id=peer, device_id_type=MESH
        )
        copy.start()
        sends.append(copy)

    for j, peer in enumerate(ring):
        send(p1s.at[lax.rem(peer[0], 2)], p1r.at[r], p1_ss.at[j], p1_rs.at[r], peer)
    for j, peer in enumerate(ring):
        send(p1os.at[lax.rem(peer[0], 2)], p1or.at[r], p1o_ss.at[j], p1o_rs.at[r], peer)
    p1r[r] = p1s[c]
    p1or[r] = p1os[c]

    hid_copy.wait()
    row = lax.broadcasted_iota(jnp.int32, (512, 256), 0)
    col = lax.broadcasted_iota(jnp.int32, (512, 256), 1)
    at_row = (
        lax.rem(col // 16, 4) * 128
        + lax.rem(t, 2) * 64
        + (col // 128) * 32
        + lax.rem(col // 64, 2) * 16
        + lax.rem(col, 16)
    )
    select = jnp.where(row == at_row, 1.0, 0.0).astype(BF16)
    half = pl.multiple_of((t // 2) * 128, 128)
    for g in range(4):
        wide = jnp.concatenate(
            [hid_v[:, pl.ds(pl.multiple_of((4 * g + j) * 512 + half, 128), 128)] for j in range(4)],
            axis=1,
        )
        got = jnp.dot(wide, select, preferred_element_type=F32).astype(BF16)
        low, high = got[:, 0:128], got[:, 128:256]
        hc[0, :, g * 128 : (g + 1) * 128] = jnp.where(c == 0, low, high)
        hcs[:, g * 128 : (g + 1) * 128] = jnp.where(c == 0, high, low)
    send(hcs, hc.at[1], hc_sem.at[0], hc_sem.at[1], (other, t))
    hc_copy = sends[-1]

    acc_q[...] = jnp.zeros_like(acc_q)
    acc_kv[...] = jnp.zeros_like(acc_kv)

    @pl.loop(0, K_PARTS)
    def _(i):
        for copy in q_copies(i):
            copy.wait()
        at = pl.ds(pl.multiple_of(i * rows, rows), rows)
        part = hid_v[:, at]
        acc_q[...] += jnp.dot(part, wq_v[at, :], preferred_element_type=F32)
        acc_kv[...] += jnp.dot(part, wkv_v[at, :], preferred_element_type=F32)

    for peer in ring:
        pltpu.make_async_copy(p1r.at[peer[0]], p1r.at[peer[0]], p1_rs.at[peer[0]]).wait()
    zero = jnp.zeros((16, 128), BF16)
    for s in range(R):
        of = owner[s]
        dv = p1r[of, 32:48, :]
        for h in range(2):
            at = (((s // 4) * 2 + h) * 4 + s % 4) * 16
            dc[at : at + 16, 0:128] = p1r[of, h * 16 : h * 16 + 16, :]
            keep = lane < 64 if h == 0 else lane >= 64
            dc[at : at + 16, 128:256] = jnp.where(keep, dv, zero)
    hc_copy.wait_recv()
    both = hc[...].reshape(64, 512)
    part_a = jnp.dot(both, dc[...], preferred_element_type=F32)
    packed = []
    for j in range(2):
        a = part_a[j * 32 : j * 32 + 32]
        v = a[:, 128:256]
        v = v + pltpu.roll(v, 64, 1)
        packed.append((a[:, 0:128].astype(BF16), jnp.where(lane < 64, v[0:16], v[16:32]).astype(BF16)))
    j = 0
    for i in (6, 2, 5, 3, 4, 7, 1, 0):
        to = lax.rem(t + i, T)
        first, second = p1r[owner[2 * to], 48:64, :], p1r[owner[2 * to + 1], 48:64, :]
        for dc_ in (0, 1):
            p2s[j, 0:32, :] = packed[dc_][0]
            p2s[j, 32:48, :] = packed[dc_][1]
            p2s[j, 48:64, :] = first
            p2s[j, 64:80, :] = second
            if i or dc_:
                peer = (r if dc_ == 0 else other, to)
                send(p2s.at[j], p2r.at[mine], p2_ss.at[j], p2_rs.at[mine], peer)
            else:
                p2r[mine] = p2s[j]
            j += 1

    for peer in ring:
        pltpu.make_async_copy(p1or.at[peer[0]], p1or.at[peer[0]], p1o_rs.at[peer[0]]).wait()
    j = 0
    for i in (6, 2, 5, 3, 4, 7, 1, 0):
        to = lax.rem(t + i, T)
        p2os[j, 0:32, :] = p1or[owner[2 * to]]
        p2os[j, 32:64, :] = p1or[owner[2 * to + 1]]
        for dc_ in (0, 1):
            if i or dc_:
                peer = (r if dc_ == 0 else other, to)
                send(p2os.at[j], p2or.at[mine], p2o_ss.at[2 * j + dc_], p2o_rs.at[mine], peer)
            else:
                p2or[mine] = p2os[j]
        j += 1

    k_v[:, 1040:1152, :] = jnp.zeros((8, 112, 128), BF16)
    v_v[:, 1040:1152, :] = jnp.zeros((8, 112, 128), BF16)
    kn_s[32:128, :] = jnp.zeros((96, 128), F32)
    vn_s[32:128, :] = jnp.zeros((96, 128), F32)
    uqk[0:64, 512:640] = jnp.zeros((64, 128), BF16)
    uqk[64:128, 0:512] = jnp.zeros((64, 512), BF16)

    for i in range(T):
        for dc_ in (0, 1):
            if i or dc_:
                m = lax.rem(t + i, T) * 2 + (c if dc_ == 0 else 1 - c)
                pltpu.make_async_copy(p2r.at[m], p2r.at[m], p2_rs.at[m]).wait()
    a_qk = jnp.zeros((32, 128), F32)
    a_v = jnp.zeros((16, 128), F32)
    for m in range(16):
        a_qk = a_qk + p2r[m, 0:32, :].astype(F32)
        a_v = a_v + p2r[m, 32:48, :].astype(F32)
    for m in range(12):
        g, block = m % 4, m // 4
        first, second = p2r[m, 48:64, :], p2r[m, 64:80, :]
        if block < 2:
            uqk[g * 16 : g * 16 + 16, block * 128 : block * 128 + 128] = first
            uqk[g * 16 : g * 16 + 16, 256 + block * 128 : 384 + block * 128] = second
        else:
            first, second = first.astype(F32), second.astype(F32)
            uk = jnp.where(lane < 64, first, pltpu.roll(second, 64, 1)).astype(BF16)
            uvt = jnp.where(lane < 64, pltpu.roll(first, 64, 1), second).astype(BF16)
            uqk[64 + g * 16 : 80 + g * 16, 512:640] = uk
            uv[g * 16 : g * 16 + 16, :] = uvt
            uv[64 + g * 16 : 80 + g * 16, :] = uvt
    a_v2 = jnp.concatenate([jnp.where(lane < 64, a_v, 0.0), jnp.where(lane >= 64, a_v, 0.0)], axis=0)
    d_qk = jnp.dot(a_qk.astype(BF16), uqk[...], preferred_element_type=F32)
    d_val = jnp.dot(a_v2.astype(BF16), uv[...], preferred_element_type=F32)
    q = (acc_q[...] + SCALE * d_qk[:, 0:512]).astype(BF16).astype(F32)
    for s in range(4):
        for h in range(4):
            q_s[(s * 4 + h) * 8 : (s * 4 + h) * 8 + 8, :] = q[s * 8 : s * 8 + 8, h * 128 : h * 128 + 128]
    kn_s[0:32, :] = acc_kv[:, 0:128] + SCALE * d_qk[:, 512:640]
    vn_s[0:32, :] = acc_kv[:, 128:256] + SCALE * d_val

    for copy in cache:
        copy.wait()
    where = lax.broadcasted_iota(jnp.int32, (16, 1152), 1)
    step = lax.broadcasted_iota(jnp.int32, (16, 1152), 0) // 4
    fresh = jnp.logical_and(where >= 1024, where - 1024 <= step)
    factor = math.log2(math.e) / math.sqrt(HEAD_DIM)
    for b in range(8):
        k_v[b, 1024:1040, :] = kn_s[pl.ds(b, 16, stride=8), :].astype(BF16)
        v_v[b, 1024:1040, :] = vn_s[pl.ds(b, 16, stride=8), :].astype(BF16)
    for b in range(8):
        qb = q_s[pl.ds(b, 16, stride=8), :].astype(BF16)
        scores = lax.dot_general(qb, k_v[b], (((1,), (1,)), ((), ())), preferred_element_type=F32)
        seen = jnp.logical_or(where < lengths[b], fresh)
        scores = jnp.where(seen, scores, MASKED)
        top = jnp.max(scores, axis=-1, keepdims=True)
        weights = jnp.exp2((scores - top) * factor)
        total = jnp.sum(weights, axis=-1, keepdims=True)
        got = jnp.dot(weights.astype(BF16), v_v[b], preferred_element_type=F32)
        ctx_s[pl.ds(b, 16, stride=8), :] = got / total
    for s in range(4):
        for h in range(4):
            cx[s * 8 : s * 8 + 8, h * 128 : h * 128 + 128] = ctx_s[(s * 4 + h) * 8 : (s * 4 + h) * 8 + 8, :]
    context = cx[...].astype(BF16)

    for i in range(T):
        for dc_ in (0, 1):
            if i or dc_:
                m = lax.rem(t + i, T) * 2 + (c if dc_ == 0 else 1 - c)
                pltpu.make_async_copy(p2or.at[m], p2or.at[m], p2o_rs.at[m]).wait()
    for m in range(16):
        g, block = m % 4, m // 4
        for j in range(2):
            tile = p2or[m, j * 32 : j * 32 + 16, :]
            at = j * 512 + block * 128
            uo_v[g * 16 : g * 16 + 16, at : at + 128] = tile
            uo_v[64 + g * 16 : 80 + g * 16, at : at + 128] = tile
            if m < 8:
                do_v[j, m * 16 : m * 16 + 16, :] = p2or[m, j * 32 + 16 : j * 32 + 32, :]
    lane32 = lax.broadcasted_iota(jnp.int32, (32, 128), 1)
    z_low = jnp.dot(context[:, 0:128], do_v[0], preferred_element_type=F32)
    z_low += jnp.dot(context[:, 256:384], do_v[1], preferred_element_type=F32)
    z_high = jnp.dot(context[:, 128:256], do_v[0], preferred_element_type=F32)
    z_high += jnp.dot(context[:, 384:512], do_v[1], preferred_element_type=F32)
    z = jnp.where(lane32 < 64, z_low, z_high)
    z_sent = z.astype(BF16)

    own = None
    for i in range(T):
        wo_copies[i].wait()
        part = jnp.dot(context, wo_v[i], preferred_element_type=F32)
        if i < T - 1:
            rss[i, :, 0:1024] = part.astype(BF16)
            rss[i, :, 1024:1152] = z_sent
            send(rss.at[i], rsr.at[t], rs_ss.at[i], rs_rs.at[t], (r, heads[i]))
        else:
            own = part
    for i in range(1, T):
        m = lax.rem(t + i, T)
        pltpu.make_async_copy(rsr.at[m], rsr.at[m], rs_rs.at[m]).wait()
        own = own + rsr[m, :, 0:1024].astype(F32)
        z = z + rsr[m, :, 1024:1152].astype(F32)
    own = own + SCALE * jnp.dot(z.astype(BF16), uo_v[...], preferred_element_type=F32)
    out_ref[...] = own.astype(BF16)
    for copy in sends:
        copy.wait_send()


def body(
    hidden, query_weight, keyval_weight, output_weight, adapter_down_stack, adapter_query_up,
    adapter_keyval_up, adapter_output_down, adapter_output_up, owner, key_cache_rows, value_cache_rows, lengths,
):
    steps, batch, width = hidden.shape
    rows = steps * batch
    anywhere = pl.BlockSpec(memory_space=pl.ANY)
    scalars = pl.BlockSpec(memory_space=pltpu.SMEM)
    dma = pltpu.SemaphoreType.DMA
    out = pl.pallas_call(
        kernel,
        out_shape=jax.ShapeDtypeStruct((rows, 1024), BF16),
        in_specs=[scalars, scalars] + [anywhere] * 11,
        out_specs=pl.BlockSpec(memory_space=pltpu.VMEM),
        scratch_shapes=[
            pltpu.VMEM((32, 8192), BF16),
            pltpu.VMEM((8192, 512), BF16),
            pltpu.VMEM((8192, 256), BF16),
            pltpu.VMEM((8, 512, 1024), BF16),
            pltpu.VMEM((8, 1152, 128), BF16),
            pltpu.VMEM((8, 1152, 128), BF16),
            pltpu.VMEM((3, 64, 64), BF16),
            pltpu.VMEM((64, 256), BF16),
            pltpu.VMEM((2, 64, 64), BF16),
            pltpu.VMEM((256, 64), BF16),
            pltpu.VMEM((64, 512), BF16),
            pltpu.VMEM((4, 64, 128), BF16),
            pltpu.VMEM((128, 128), BF16),
            pltpu.VMEM((2, 64, 128), BF16),
            pltpu.VMEM((16, 64, 128), BF16),
            pltpu.VMEM((2, 32, 128), BF16),
            pltpu.VMEM((16, 32, 128), BF16),
            pltpu.VMEM((2, 32, 512), BF16),
            pltpu.VMEM((32, 512), BF16),
            pltpu.VMEM((512, 256), BF16),
            pltpu.VMEM((16, 80, 128), BF16),
            pltpu.VMEM((16, 80, 128), BF16),
            pltpu.VMEM((8, 64, 128), BF16),
            pltpu.VMEM((16, 64, 128), BF16),
            pltpu.VMEM((128, 640), BF16),
            pltpu.VMEM((128, 128), BF16),
            pltpu.VMEM((128, 128), F32),
            pltpu.VMEM((128, 128), F32),
            pltpu.VMEM((128, 128), F32),
            pltpu.VMEM((32, 512), F32),
            pltpu.VMEM((32, 256), F32),
            pltpu.VMEM((128, 128), F32),
            pltpu.VMEM((32, 512), F32),
            pltpu.VMEM((2, 128, 128), BF16),
            pltpu.VMEM((128, 1024), BF16),
            pltpu.VMEM((8, 32, 1152), BF16),
            pltpu.VMEM((8, 32, 1152), BF16),
            dma((6,)), dma((K_PARTS,)), dma((2, K_PARTS)), dma((2,)), dma((T,)), dma((2,)),
            dma((15,)), dma((R,)), dma((15,)), dma((R,)), dma((16,)), dma((16,)), dma((16,)), dma((16,)),
            dma((T,)), dma((T,)),
        ],
        compiler_params=pltpu.CompilerParams(
            collective_id=0, has_side_effects=True, vmem_limit_bytes=60 * 1024 * 1024
        ),
        name="adapter_attention",
    )(
        owner, lengths, hidden.reshape(rows, width), query_weight, keyval_weight, output_weight,
        adapter_down_stack, adapter_query_up, adapter_keyval_up, adapter_output_down, adapter_output_up,
        key_cache_rows, value_cache_rows,
    )
    return out.reshape(steps, batch, 1024)


def solution(mesh):
    in_specs = (
        P(None, "replica", None),
        P(None, "tensor"),
        P(None, None, "tensor"),
        P("tensor", None),
        P(None, "replica", None),
        P(None, "replica"),
        P(None, None, "replica"),
        P("replica", None),
        P(None, "replica"),
        P(),
        P("replica", None, "tensor"),
        P("replica", None, "tensor"),
        P("replica"),
    )
    out_specs = P(None, "replica", "tensor")
    return jax.shard_map(body, mesh=mesh, in_specs=in_specs, out_specs=out_specs, check_vma=False)
```

time: 534 us -> 45.2 us (0.08)
  waiting for transfers between devices: 350 us -> 0 us
  local copies, waits for them, and re-layouts: 70 us -> 4.8 us
  blocking collectives: 61.3 us -> 0 us
  Pallas kernels: 0 us -> 40.1 us
  matrix products: 18.1 us -> 0 us
  other arithmetic: 16.9 us -> 0 us
  between operations: 14.4 us -> 0.01 us
    reduce_scatter x4 -> x0, waiting for transfers between devices: 283 us -> none  [body(): lax.psum_scatter(partial_sums[position].astype(jnp.bfloat16), 'tensor', s...]
    all_gather x3 -> x0, waiting for transfers between devices: 64.7 us -> none  [the longest x1 34.5 us: body(): lax.all_gather(out_cols, 'replica', axis=1, tiled=True)]
    all_gather x3 -> x0, blocking collectives: 61.3 us -> none  [the longest x1 22.9 us: body(): lax.all_gather(adapter_keyval_up, 'replica', axis=2, tiled=True)]
    pallas_call x0 -> x1, Pallas kernels: none -> 40.1 us  [body(): pl.pallas_call(kernel, out_shape=jax.ShapeDtypeStruct((rows, 1024), BF16)...]
    reshape x6 -> x0, local copies, waits for them, and re-layouts: 26.5 us -> none  [recover_weight(): blocks = jnp.take(stored.reshape(block_shape), owner, axis=reduce_axis)]
    gather x10 -> x0, local copies, waits for them, and re-layouts: 26.1 us -> none  [recover_weight(): blocks = jnp.take(stored.reshape(block_shape), owner, axis=reduce_axis)]
    dot_general x11 -> x0, matrix products: 18.1 us -> none  [the longest x4 6.32 us: combine_block(): jnp.dot(down_factor, up_factor, preferred_element_type=jnp.float32)]
    select_n x4 -> x0, other arithmetic: 13.5 us -> none  [recover_weight(): blocks = jnp.take(stored.reshape(block_shape), owner, axis=reduce_axis)]
  transfers between devices with their start and end apart: 7 -> 0, of which waited for: 6 -> 0; matrix products, arithmetic and copies ran while one was open for 8% -> 0% of each run, Pallas kernels for 0% -> 0%
where the time goes in v1:
time: 45.2 us; the launch traced here: 44.9 us
  Pallas kernels  40.1 us (89%)
  local copies, waits for them, and re-layouts  4.8 us (11%)
    pallas_call x1, Pallas kernels, body(): pl.pallas_call(kernel, out_shape=jax.ShapeDtypeStruct((rows, 1024), BF16)...  40.1 us
    unnamed x3, local copies, waits for them, and re-layouts  4.8 us

profile of v1, /device:TPU:1, one launch (start us, length us, event | category | flops | bytes accessed | tf_op | source)
XLA Modules:
  0.0 44.9 jit_solution(9542907766728234734)
XLA Ops:
  0.0 1.5 %copy.15.odn = bf16[256,64]{1,0:T(8,128)(2,1)} copy(bf16[256,64]{0,1:T(8,128)(2,1)} %param.20) | data formatting | bytes 65536 | tf_op args[7]
  1.5 1.8 %copy.14.dstk = bf16[3,512,64]{2,1,0:T(8,128)(2,1)} copy(bf16[3,512,64]{1,2,0:T(8,128)(2,1)} %param.17) | data formatting | bytes 393216 | tf_op args[4]
  3.3 40.1 %adapter_attention.1 = bf16[32,1024]{1,0:T(8,128)(2,1)} custom-call(s32[16]{0:T(128)} %owner.1, s32[8]{0:T(128)} %lengths.1, bf16[32,8192]{1,0:T(8,128)(2,1)} %bitcast.2, bf16[8192,512]{1,0:T(8,128)(2,1)} %wq.1, bf16[2,8192,128]{2,1,0:T(8,128)(2,1)} %wkv.1, bf16[512,8192]{1,0:T(8,128)(2,1)} %wo.1, bf16[3,512,64]{2,1,0:T(8,128)(2,1)} %copy.14.dstk, ...), custom_call_target="tpu_custom_call" | custom-call | tf_op jit(solution)/shard_map/adapter_attention/pallas_call | solution.py:336
  43.4 1.5 %copy.17 = bf16[4,8,1024]{2,1,0:T(8,128)(2,1)} copy(bf16[4,8,1024]{2,1,0:T(8,128)(2,1)} %bitcast.3) | data formatting | bytes 131072

commit v2 on v1

v2 whole, which is shorter than its diff:
```python
import math

import jax
import jax.numpy as jnp
from jax import lax
from jax.experimental import pallas as pl
from jax.experimental.pallas import tpu as pltpu
from jax.sharding import PartitionSpec as P

MESH = pl.DeviceIdType.MESH
BF16 = jnp.bfloat16
F32 = jnp.float32
HEAD_DIM = 128
SCALE = 0.5
MASKED = -1e30
R, T = 16, 8
K_PARTS = 4


def kernel(
    owner_any, lengths_any, hid, wq, wkv, wo, dstk, qup, kvup, odn, oup, kc, vc,
    out_ref,
    hid_v, wq_v, wkv_v, wo_v, k_v, v_v, d_v, d_t, qup_v, kvup_v, odn_v, oup_v, upk, odp,
    p1d, p1u, p1o, hc, dc, p2s, p2r, p2os, p2or,
    uqk, uv, q_s, kn_s, vn_s, acc_q, acc_kv, ctx_s, cx, do_v, uo_v, rss, rsr, zs, zr,
    owner, lengths, small_sem, q_sem, kv_sem, cache_sem, wo_sem,
    p1d_ss, p1d_rs, p1u_ss, p1u_rs, p1o_ss, p1o_rs, fwd_ss, fwd_rs, p2_ss, p2_rs, p2o_ss, p2o_rs,
    rs_ss, rs_rs, z_ss, z_rs,
):
    r, t = lax.axis_index("replica"), lax.axis_index("tensor")
    x, zl, c = r // 4, lax.rem(r // 2, 2), lax.rem(r, 2)
    zh, y = t // 4, lax.rem(t, 4)
    other = (r + 1 - 2 * c, t)
    mine = c * 8 + r // 2
    rows = 8192 // K_PARTS
    ring = [
        (lax.rem(x + dx, 4) * 4 + (zl if dz == 0 else 1 - zl) * 2 + c, t)
        for dx, dz in ((2, 1), (1, 1), (3, 1), (2, 0), (1, 0), (3, 0), (0, 1))
    ]
    slots = [c * 8 + peer[0] // 2 for peer in ring]
    heads = [
        (zh if dz == 0 else 1 - zh) * 4 + lax.rem(y + dy, 4)
        for dz, dy in ((1, 2), (1, 1), (1, 3), (0, 2), (1, 0), (0, 1), (0, 3), (0, 0))
    ]
    cross = [(r, to) for to in heads[:-1]]

    barrier = pltpu.get_barrier_semaphore()
    greeted = ring + [other] + cross
    for peer in greeted:
        pl.semaphore_signal(barrier, inc=1, device_id=peer, device_id_type=MESH)

    t128 = pl.multiple_of((t // 2) * 128, 128)
    small = [
        pltpu.make_async_copy(dstk.at[:, :, pl.ds(t128, 128)], d_v, small_sem.at[0]),
        pltpu.make_async_copy(qup, qup_v, small_sem.at[1]),
        pltpu.make_async_copy(kvup, kvup_v, small_sem.at[2]),
        pltpu.make_async_copy(odn, odn_v, small_sem.at[3]),
        pltpu.make_async_copy(oup, oup_v, small_sem.at[4]),
    ]
    hid_copy = pltpu.make_async_copy(hid, hid_v, small_sem.at[5])
    scalars = [
        pltpu.make_async_copy(owner_any, owner, small_sem.at[6]),
        pltpu.make_async_copy(lengths_any, lengths, small_sem.at[7]),
    ]
    for copy in small:
        copy.start()
    hid_copy.start()
    for copy in scalars:
        copy.start()

    def q_copies(i):
        at = pl.ds(pl.multiple_of(i * rows, rows), rows)
        return [
            pltpu.make_async_copy(wq.at[at, :], wq_v.at[at, :], q_sem.at[i]),
            pltpu.make_async_copy(wkv.at[0, at, :], wkv_v.at[at, pl.ds(0, 128)], kv_sem.at[0, i]),
            pltpu.make_async_copy(wkv.at[1, at, :], wkv_v.at[at, pl.ds(128, 128)], kv_sem.at[1, i]),
        ]

    for i in range(K_PARTS):
        for copy in q_copies(i):
            copy.start()

    k_v[:, 1040:1152, :] = jnp.zeros((8, 112, 128), BF16)
    v_v[:, 1040:1152, :] = jnp.zeros((8, 112, 128), BF16)
    kn_s[32:128, :] = jnp.zeros((96, 128), F32)
    vn_s[32:128, :] = jnp.zeros((96, 128), F32)
    uqk[0:64, 512:640] = jnp.zeros((64, 128), BF16)
    uqk[64:128, 0:512] = jnp.zeros((64, 512), BF16)

    for copy in small:
        copy.wait()
    lane = lax.broadcasted_iota(jnp.int32, (32, 128), 1)
    d_t[0] = jnp.concatenate([d_v[0], d_v[1]], axis=0).T
    d_t[1] = jnp.concatenate([d_v[2], d_v[2]], axis=0).T
    t64 = pl.multiple_of(lax.rem(t, 2) * 64, 64)
    p1d[mine, 0:64, :] = d_t[0, pl.ds(t64, 64), :]
    v_rows = d_t[1, pl.ds(t64, 64), :]
    p1d[mine, 64:96, :] = jnp.where(lane < 64, v_rows[0:32], v_rows[32:64])
    upk[0] = qup_v[:, 0:128]
    upk[1] = qup_v[:, 128:256]
    upk[2] = jnp.concatenate([kvup_v[0], kvup_v[1]], axis=1)
    upk[3] = jnp.zeros((64, 128), BF16)
    t32 = pl.multiple_of(lax.rem(t, 2) * 32, 32)
    p1u[mine] = upk[t // 2, pl.ds(t32, 32), :]
    odp[0:64, :] = odn_v[:, 0:128]
    odp[64:128, :] = odn_v[:, 128:256]
    p1o[mine, 0:32, :] = oup_v[pl.ds(t32, 32), pl.ds(t128, 128)]
    p1o[mine, 32:48, :] = odp[pl.ds(pl.multiple_of(t * 16, 16), 16), :]

    pl.semaphore_wait(barrier, len(greeted))

    sends = []

    def send(src, dst, ss, rs, peer):
        copy = pltpu.make_async_remote_copy(
            src_ref=src, dst_ref=dst, send_sem=ss, recv_sem=rs, device_id=peer, device_id_type=MESH
        )
        copy.start()
        sends.append(copy)

    def arrived(ref, sem):
        pltpu.make_async_copy(ref, ref, sem).wait()

    for j, peer in enumerate(ring):
        send(p1d.at[mine], p1d.at[mine], p1d_ss.at[j], p1d_rs.at[mine], peer)
    for j, peer in enumerate(ring):
        send(p1u.at[mine], p1u.at[mine], p1u_ss.at[j], p1u_rs.at[mine], peer)
    send(p1d.at[mine], p1d.at[mine], p1d_ss.at[7], p1d_rs.at[mine], other)

    cache = [
        pltpu.make_async_copy(kc, k_v.at[:, pl.ds(0, 1024), :], cache_sem.at[0]),
        pltpu.make_async_copy(vc, v_v.at[:, pl.ds(0, 1024), :], cache_sem.at[1]),
    ]
    for copy in cache:
        copy.start()
    wo_copies = [
        pltpu.make_async_copy(
            wo.at[:, pl.ds(pl.multiple_of(heads[i] * 1024, 1024), 1024)], wo_v.at[i], wo_sem.at[i]
        )
        for i in range(T)
    ]
    for copy in wo_copies:
        copy.start()

    hid_copy.wait()
    odd = lax.rem(t, 2) == 1
    for g in range(8):
        first = hid_v[:, pl.ds(pl.multiple_of((2 * g) * 512 + t128, 128), 128)].astype(F32)
        second = hid_v[:, pl.ds(pl.multiple_of((2 * g + 1) * 512 + t128, 128), 128)].astype(F32)
        low = jnp.where(lane < 64, first, pltpu.roll(second, 64, 1))
        high = jnp.where(lane < 64, pltpu.roll(first, 64, 1), second)
        hc[:, g * 128 : (g + 1) * 128] = jnp.where(odd, high, low).astype(BF16)

    acc_q[...] = jnp.zeros_like(acc_q)
    acc_kv[...] = jnp.zeros_like(acc_kv)

    @pl.loop(0, K_PARTS)
    def _(i):
        for copy in q_copies(i):
            copy.wait()
        at = pl.ds(pl.multiple_of(i * rows, rows), rows)
        part = hid_v[:, at]
        acc_q[...] += jnp.dot(part, wq_v[at, :], preferred_element_type=F32)
        acc_kv[...] += jnp.dot(part, wkv_v[at, :], preferred_element_type=F32)

    for j, peer in enumerate(ring):
        send(p1o.at[mine], p1o.at[mine], p1o_ss.at[j], p1o_rs.at[mine], peer)

    same = pl.ds(pl.multiple_of(c * 8, 8), 8)
    for j, slot in reversed(list(enumerate(slots))):
        arrived(p1d.at[slot], p1d_rs.at[slot])
        send(p1d.at[slot], p1d.at[slot], p1d_ss.at[8 + j], p1d_rs.at[slot], other)
    for slot in slots:
        arrived(p1u.at[slot], p1u_rs.at[slot])
    send(p1u.at[same], p1u.at[same], fwd_ss.at[0], fwd_rs.at[0], other)
    u_copy = sends[-1]

    for copy in scalars:
        copy.wait()

    for i in range(8):
        slot = (1 - c) * 8 + i
        arrived(p1d.at[slot], p1d_rs.at[slot])

    def slot_of(s):
        return lax.rem(owner[s], 2) * 8 + owner[s] // 2

    zero = jnp.zeros((32, 128), BF16)
    for s in range(R):
        of = slot_of(s)
        dc[s * 64 : s * 64 + 64, 0:128] = p1d[of, 0:64, :]
        dv = p1d[of, 64:96, :]
        dc[s * 64 : s * 64 + 32, 128:256] = jnp.where(lane < 64, dv, zero)
        dc[s * 64 + 32 : s * 64 + 64, 128:256] = jnp.where(lane < 64, zero, dv)
    part_a = jnp.dot(hc[...], dc[...], preferred_element_type=F32)
    part_v = part_a[:, 128:256]
    part_v = part_v + pltpu.roll(part_v, 64, 1)
    part_qk = part_a[:, 0:128].astype(BF16)
    part_v = jnp.where(lane[0:16] < 64, part_v[0:16], part_v[16:32]).astype(BF16)
    u_copy.wait_recv()
    for j, to in enumerate(heads):
        p2s[j, 0:32, :] = part_qk
        p2s[j, 32:48, :] = part_v
        p2s[j, 48:80, :] = p1u[slot_of(2 * to)]
        p2s[j, 80:112, :] = p1u[slot_of(2 * to + 1)]
        if j < 7:
            send(p2s.at[j], p2r.at[t], p2_ss.at[j], p2_rs.at[t], cross[j])
        else:
            p2r[t] = p2s[j]

    for slot in slots:
        arrived(p1o.at[slot], p1o_rs.at[slot])
    send(p1o.at[same], p1o.at[same], fwd_ss.at[1], fwd_rs.at[1], other)
    sends[-1].wait_recv()
    for j, to in enumerate(heads):
        p2os[j, 0:48, :] = p1o[slot_of(2 * to)]
        p2os[j, 48:96, :] = p1o[slot_of(2 * to + 1)]
        if j < 7:
            send(p2os.at[j], p2or.at[t], p2o_ss.at[j], p2o_rs.at[t], cross[j])
        else:
            p2or[t] = p2os[j]

    for m in reversed(heads[:-1]):
        arrived(p2r.at[m], p2_rs.at[m])
    a_qk = jnp.zeros((32, 128), F32)
    a_v = jnp.zeros((16, 128), F32)
    for m in range(T):
        a_qk = a_qk + p2r[m, 0:32, :].astype(F32)
        a_v = a_v + p2r[m, 32:48, :].astype(F32)
    for m in range(6):
        g, block = (m % 2) * 32, m // 2
        first, second = p2r[m, 48:80, :], p2r[m, 80:112, :]
        if block < 2:
            uqk[g : g + 32, block * 128 : block * 128 + 128] = first
            uqk[g : g + 32, 256 + block * 128 : 384 + block * 128] = second
        else:
            first, second = first.astype(F32), second.astype(F32)
            uk = jnp.where(lane < 64, first, pltpu.roll(second, 64, 1)).astype(BF16)
            uvt = jnp.where(lane < 64, pltpu.roll(first, 64, 1), second).astype(BF16)
            uqk[64 + g : 96 + g, 512:640] = uk
            uv[g : g + 32, :] = uvt
            uv[64 + g : 96 + g, :] = uvt
    low = lane[0:16] < 64
    a_v2 = jnp.concatenate([jnp.where(low, a_v, 0.0), jnp.where(low, 0.0, a_v)], axis=0)
    d_qk = jnp.dot(a_qk.astype(BF16), uqk[...], preferred_element_type=F32)
    d_val = jnp.dot(a_v2.astype(BF16), uv[...], preferred_element_type=F32)
    q = (acc_q[...] + SCALE * d_qk[:, 0:512]).astype(BF16).astype(F32)
    for s in range(4):
        for h in range(4):
            q_s[(s * 4 + h) * 8 : (s * 4 + h) * 8 + 8, :] = q[s * 8 : s * 8 + 8, h * 128 : h * 128 + 128]
    kn_s[0:32, :] = acc_kv[:, 0:128] + SCALE * d_qk[:, 512:640]
    vn_s[0:32, :] = acc_kv[:, 128:256] + SCALE * d_val

    for copy in cache:
        copy.wait()
    where = lax.broadcasted_iota(jnp.int32, (16, 1152), 1)
    step = lax.broadcasted_iota(jnp.int32, (16, 1152), 0) // 4
    fresh = jnp.logical_and(where >= 1024, where - 1024 <= step)
    factor = math.log2(math.e) / math.sqrt(HEAD_DIM)
    for b in range(8):
        k_v[b, 1024:1040, :] = kn_s[pl.ds(b, 16, stride=8), :].astype(BF16)
        v_v[b, 1024:1040, :] = vn_s[pl.ds(b, 16, stride=8), :].astype(BF16)
    for b in range(8):
        qb = q_s[pl.ds(b, 16, stride=8), :].astype(BF16)
        scores = lax.dot_general(qb, k_v[b], (((1,), (1,)), ((), ())), preferred_element_type=F32)
        seen = jnp.logical_or(where < lengths[b], fresh)
        scores = jnp.where(seen, scores, MASKED)
        top = jnp.max(scores, axis=-1, keepdims=True)
        weights = jnp.exp2((scores - top) * factor)
        total = jnp.sum(weights, axis=-1, keepdims=True)
        got = jnp.dot(weights.astype(BF16), v_v[b], preferred_element_type=F32)
        ctx_s[pl.ds(b, 16, stride=8), :] = got / total
    for s in range(4):
        for h in range(4):
            cx[s * 8 : s * 8 + 8, h * 128 : h * 128 + 128] = ctx_s[(s * 4 + h) * 8 : (s * 4 + h) * 8 + 8, :]
    context = cx[...].astype(BF16)

    for m in reversed(heads[:-1]):
        arrived(p2or.at[m], p2o_rs.at[m])
    for m in range(T):
        g, block = (m % 2) * 32, m // 2
        for j in range(2):
            tile = p2or[m, j * 48 : j * 48 + 32, :]
            at = j * 512 + block * 128
            uo_v[g : g + 32, at : at + 128] = tile
            uo_v[64 + g : 96 + g, at : at + 128] = tile
            do_v[m * 16 : m * 16 + 16, j * 128 : j * 128 + 128] = p2or[m, j * 48 + 32 : j * 48 + 48, :]
    halves = jnp.concatenate(
        [
            jnp.concatenate([context[:, 0:128], context[:, 128:256]], axis=0),
            jnp.concatenate([context[:, 256:384], context[:, 384:512]], axis=0),
        ],
        axis=1,
    )
    z_all = lax.dot_general(halves, do_v[...], (((1,), (1,)), ((), ())), preferred_element_type=F32)
    z = jnp.where(lane < 64, z_all[0:32], z_all[32:64])
    zs[...] = z.astype(BF16)
    for j, peer in enumerate(cross):
        send(zs, zr.at[t], z_ss.at[j], z_rs.at[t], peer)

    own = None
    for i in range(T):
        wo_copies[i].wait()
        part = jnp.dot(context, wo_v[i], preferred_element_type=F32)
        if i < T - 1:
            rss[i] = part.astype(BF16)
            send(rss.at[i], rsr.at[t], rs_ss.at[i], rs_rs.at[t], cross[i])
        else:
            own = part
    for m in reversed(heads[:-1]):
        arrived(zr.at[m], z_rs.at[m])
        z = z + zr[m].astype(F32)
    own = own + SCALE * jnp.dot(z.astype(BF16), uo_v[...], preferred_element_type=F32)
    for m in reversed(heads[:-1]):
        arrived(rsr.at[m], rs_rs.at[m])
        own = own + rsr[m].astype(F32)
    out_ref[...] = own.astype(BF16)
    for copy in sends:
        copy.wait_send()


def body(
    hidden, query_weight, keyval_weight, output_weight, adapter_down_stack, adapter_query_up,
    adapter_keyval_up, adapter_output_down, adapter_output_up, owner, key_cache_rows, value_cache_rows, lengths,
):
    steps, batch, width = hidden.shape
    rows = steps * batch
    anywhere = pl.BlockSpec(memory_space=pl.ANY)
    dma = pltpu.SemaphoreType.DMA
    out = pl.pallas_call(
        kernel,
        out_shape=pltpu.VMEM((rows, 1024), BF16),
        in_specs=[anywhere] * 13,
        out_specs=pl.BlockSpec(memory_space=pltpu.VMEM),
        scratch_shapes=[
            pltpu.VMEM((32, 8192), BF16),
            pltpu.VMEM((8192, 512), BF16),
            pltpu.VMEM((8192, 256), BF16),
            pltpu.VMEM((8, 512, 1024), BF16),
            pltpu.VMEM((8, 1152, 128), BF16),
            pltpu.VMEM((8, 1152, 128), BF16),
            pltpu.VMEM((3, 64, 128), BF16),
            pltpu.VMEM((2, 128, 128), BF16),
            pltpu.VMEM((64, 256), BF16),
            pltpu.VMEM((2, 64, 64), BF16),
            pltpu.VMEM((64, 256), BF16),
            pltpu.VMEM((64, 512), BF16),
            pltpu.VMEM((4, 64, 128), BF16),
            pltpu.VMEM((128, 128), BF16),
            pltpu.VMEM((16, 96, 128), BF16),
            pltpu.VMEM((16, 32, 128), BF16),
            pltpu.VMEM((16, 48, 128), BF16),
            pltpu.VMEM((32, 1024), BF16),
            pltpu.VMEM((1024, 256), BF16),
            pltpu.VMEM((8, 112, 128), BF16),
            pltpu.VMEM((8, 112, 128), BF16),
            pltpu.VMEM((8, 96, 128), BF16),
            pltpu.VMEM((8, 96, 128), BF16),
            pltpu.VMEM((128, 640), BF16),
            pltpu.VMEM((128, 128), BF16),
            pltpu.VMEM((128, 128), F32),
            pltpu.VMEM((128, 128), F32),
            pltpu.VMEM((128, 128), F32),
            pltpu.VMEM((32, 512), F32),
            pltpu.VMEM((32, 256), F32),
            pltpu.VMEM((128, 128), F32),
            pltpu.VMEM((32, 512), F32),
            pltpu.VMEM((128, 256), BF16),
            pltpu.VMEM((128, 1024), BF16),
            pltpu.VMEM((8, 32, 1024), BF16),
            pltpu.VMEM((8, 32, 1024), BF16),
            pltpu.VMEM((32, 128), BF16),
            pltpu.VMEM((8, 32, 128), BF16),
            pltpu.SMEM((R,), jnp.int32),
            pltpu.SMEM((8,), jnp.int32),
            dma((8,)), dma((K_PARTS,)), dma((2, K_PARTS)), dma((2,)), dma((T,)),
            dma((15,)), dma((R,)), dma((7,)), dma((R,)), dma((7,)), dma((R,)), dma((2,)), dma((2,)),
            dma((7,)), dma((T,)), dma((7,)), dma((T,)), dma((7,)), dma((T,)), dma((7,)), dma((T,)),
        ],
        compiler_params=pltpu.CompilerParams(
            collective_id=0, has_side_effects=True, vmem_limit_bytes=60 * 1024 * 1024
        ),
        name="adapter_attention",
    )(
        owner, lengths, hidden.reshape(rows, width), query_weight, keyval_weight, output_weight,
        jnp.swapaxes(adapter_down_stack, 1, 2), adapter_query_up, adapter_keyval_up, adapter_output_down.T,
        adapter_output_up, key_cache_rows, value_cache_rows,
    )
    return out.reshape(steps, batch, 1024)


def solution(mesh):
    in_specs = (
        P(None, "replica", None),
        P(None, "tensor"),
        P(None, None, "tensor"),
        P("tensor", None),
        P(None, "replica", None),
        P(None, "replica"),
        P(None, None, "replica"),
        P("replica", None),
        P(None, "replica"),
        P(),
        P("replica", None, "tensor"),
        P("replica", None, "tensor"),
        P("replica"),
    )
    out_specs = P(None, "replica", "tensor")
    return jax.shard_map(body, mesh=mesh, in_specs=in_specs, out_specs=out_specs, check_vma=False)
```

time: 45.2 us -> 35.8 us (0.79)
  Pallas kernels: 40.1 us -> 35.1 us
  local copies, waits for them, and re-layouts: 4.8 us -> 0.63 us
    pallas_call x1, Pallas kernels: 40.1 us -> 35.1 us  [body(): pl.pallas_call(kernel, out_shape=pltpu.VMEM((rows, 1024), BF16), in_specs...]
    unnamed x3 -> x1, local copies, waits for them, and re-layouts: 4.8 us -> 0.63 us
where the time goes in v2:
time: 35.8 us; the launch traced here: 35.7 us
  Pallas kernels  35.1 us (98%)
  local copies, waits for them, and re-layouts  0.63 us (2%)
    pallas_call x1, Pallas kernels, body(): pl.pallas_call(kernel, out_shape=pltpu.VMEM((rows, 1024), BF16), in_specs...  35.1 us

profile of v2, /device:TPU:1, one launch (start us, length us, event | category | flops | bytes accessed | tf_op | source)
XLA Modules:
  0.0 35.7 jit_solution(16232835457236756263)
XLA Ops:
  0.0 35.1 %adapter_attention.1 = bf16[32,1024]{1,0:T(8,128)(2,1)S(1)} custom-call(s32[16]{0:T(128)} %owner_any.1, s32[8]{0:T(128)} %lengths_any.1, bf16[32,8192]{1,0:T(8,128)(2,1)} %bitcast.5, bf16[8192,512]{1,0:T(8,128)(2,1)} %wq.1, bf16[2,8192,128]{2,1,0:T(8,128)(2,1)} %wkv.1, bf16[512,8192]{1,0:T(8,128)(2,1)} %wo.1, bf16[3,64,512]{2,1,0:T(8,128)(2,1)} %bitcast.6, ...), custom_call_target="tpu_custom_call" | custom-call | tf_op jit(solution)/shard_map/adapter_attention/pallas_call | solution.py:330
  35.1 0.6 %copy.15 = bf16[4,8,1024]{2,1,0:T(8,128)(2,1)} copy(bf16[4,8,1024]{2,1,0:T(8,128)(2,1)S(1)} %bitcast.4) | data formatting | bytes 131072

commit v3 on v2

--- a/solution.py
+++ b/solution.py
@@ -21,23 +21,22 @@
     owner_any, lengths_any, hid, wq, wkv, wo, dstk, qup, kvup, odn, oup, kc, vc,
     out_ref,
     hid_v, wq_v, wkv_v, wo_v, k_v, v_v, d_v, d_t, qup_v, kvup_v, odn_v, oup_v, upk, odp,
-    p1d, p1u, p1o, hc, dc, p2s, p2r, p2os, p2or,
-    uqk, uv, q_s, kn_s, vn_s, acc_q, acc_kv, ctx_s, cx, do_v, uo_v, rss, rsr, zs, zr,
+    p1d, p1u, p1o, hc, swap, dc, p2s, p2r, p2os, p2or,
+    uqk, uv, q_s, acc_q, acc_kv, ctx_s, cx, do_v, uo_v, rss, rsr, zs, zr,
     owner, lengths, small_sem, q_sem, kv_sem, cache_sem, wo_sem,
-    p1d_ss, p1d_rs, p1u_ss, p1u_rs, p1o_ss, p1o_rs, fwd_ss, fwd_rs, p2_ss, p2_rs, p2o_ss, p2o_rs,
-    rs_ss, rs_rs, z_ss, z_rs,
+    p1d_s, p1u_s, p1o_s, fwd_ss, fwd_rs, p2_s, p2o_s, rs_ss, rs_rs, z_s,
 ):
     r, t = lax.axis_index("replica"), lax.axis_index("tensor")
     x, zl, c = r // 4, lax.rem(r // 2, 2), lax.rem(r, 2)
     zh, y = t // 4, lax.rem(t, 4)
     other = (r + 1 - 2 * c, t)
     mine = c * 8 + r // 2
+    chip = r // 2
     rows = 8192 // K_PARTS
     ring = [
         (lax.rem(x + dx, 4) * 4 + (zl if dz == 0 else 1 - zl) * 2 + c, t)
         for dx, dz in ((2, 1), (1, 1), (3, 1), (2, 0), (1, 0), (3, 0), (0, 1))
     ]
-    slots = [c * 8 + peer[0] // 2 for peer in ring]
     heads = [
         (zh if dz == 0 else 1 - zh) * 4 + lax.rem(y + dy, 4)
         for dz, dy in ((1, 2), (1, 1), (1, 3), (0, 2), (1, 0), (0, 1), (0, 3), (0, 0))
@@ -80,10 +79,8 @@
         for copy in q_copies(i):
             copy.start()
 
-    k_v[:, 1040:1152, :] = jnp.zeros((8, 112, 128), BF16)
-    v_v[:, 1040:1152, :] = jnp.zeros((8, 112, 128), BF16)
-    kn_s[32:128, :] = jnp.zeros((96, 128), F32)
-    vn_s[32:128, :] = jnp.zeros((96, 128), F32)
+    k_v[:, 1056:1152, :] = jnp.zeros((4, 96, 256), BF16)
+    v_v[:, 1056:1152, :] = jnp.zeros((4, 96, 256), BF16)
     uqk[0:64, 512:640] = jnp.zeros((64, 128), BF16)
     uqk[64:128, 0:512] = jnp.zeros((64, 512), BF16)
 
@@ -93,9 +90,9 @@
     d_t[0] = jnp.concatenate([d_v[0], d_v[1]], axis=0).T
     d_t[1] = jnp.concatenate([d_v[2], d_v[2]], axis=0).T
     t64 = pl.multiple_of(lax.rem(t, 2) * 64, 64)
-    p1d[mine, 0:64, :] = d_t[0, pl.ds(t64, 64), :]
+    p1d[chip, 0:64, :] = d_t[0, pl.ds(t64, 64), :]
     v_rows = d_t[1, pl.ds(t64, 64), :]
-    p1d[mine, 64:96, :] = jnp.where(lane < 64, v_rows[0:32], v_rows[32:64])
+    p1d[chip, 64:96, :] = jnp.where(lane < 64, v_rows[0:32], v_rows[32:64])
     upk[0] = qup_v[:, 0:128]
     upk[1] = qup_v[:, 128:256]
     upk[2] = jnp.concatenate([kvup_v[0], kvup_v[1]], axis=1)
@@ -111,25 +108,28 @@
 
     sends = []
 
-    def send(src, dst, ss, rs, peer):
+    def send(src, dst, ss, rs, peer, late=False):
         copy = pltpu.make_async_remote_copy(
             src_ref=src, dst_ref=dst, send_sem=ss, recv_sem=rs, device_id=peer, device_id_type=MESH
         )
         copy.start()
-        sends.append(copy)
+        if not late:
+            sends.append(copy)
 
     def arrived(ref, sem):
         pltpu.make_async_copy(ref, ref, sem).wait()
 
     for j, peer in enumerate(ring):
-        send(p1d.at[mine], p1d.at[mine], p1d_ss.at[j], p1d_rs.at[mine], peer)
+        send(p1d.at[chip], p1d.at[chip], p1d_s.at[0], p1d_s.at[1], peer, late=True)
     for j, peer in enumerate(ring):
-        send(p1u.at[mine], p1u.at[mine], p1u_ss.at[j], p1u_rs.at[mine], peer)
-    send(p1d.at[mine], p1d.at[mine], p1d_ss.at[7], p1d_rs.at[mine], other)
+        send(p1u.at[mine], p1u.at[mine], p1u_s.at[0], p1u_s.at[1], peer, late=True)
 
     cache = [
-        pltpu.make_async_copy(kc, k_v.at[:, pl.ds(0, 1024), :], cache_sem.at[0]),
-        pltpu.make_async_copy(vc, v_v.at[:, pl.ds(0, 1024), :], cache_sem.at[1]),
+        pltpu.make_async_copy(
+            ref.at[b], to.at[b // 2, pl.ds(0, 1024), pl.ds(b % 2 * 128, 128)], cache_sem.at[j]
+        )
+        for j, ref, to in ((0, kc, k_v), (1, vc, v_v))
+        for b in range(8)
     ]
     for copy in cache:
         copy.start()
@@ -149,7 +149,10 @@
         second = hid_v[:, pl.ds(pl.multiple_of((2 * g + 1) * 512 + t128, 128), 128)].astype(F32)
         low = jnp.where(lane < 64, first, pltpu.roll(second, 64, 1))
         high = jnp.where(lane < 64, pltpu.roll(first, 64, 1), second)
-        hc[:, g * 128 : (g + 1) * 128] = jnp.where(odd, high, low).astype(BF16)
+        hc[0, :, g * 128 : (g + 1) * 128] = jnp.where(odd, high, low).astype(BF16)
+
+    send(hc.at[0], hc.at[1], fwd_ss.at[2], fwd_rs.at[2], other)
+    hc_copy = sends[-1]
 
     acc_q[...] = jnp.zeros_like(acc_q)
     acc_kv[...] = jnp.zeros_like(acc_kv)
@@ -164,39 +167,46 @@
         acc_kv[...] += jnp.dot(part, wkv_v[at, :], preferred_element_type=F32)
 
     for j, peer in enumerate(ring):
-        send(p1o.at[mine], p1o.at[mine], p1o_ss.at[j], p1o_rs.at[mine], peer)
+        send(p1o.at[mine], p1o.at[mine], p1o_s.at[0], p1o_s.at[1], peer, late=True)
+
+    for copy in scalars:
+        copy.wait()
+
+    arrived(p1d.at[pl.ds(0, 7)], p1d_s.at[1])
+    zero = jnp.zeros((32, 128), BF16)
+    for s in range(R):
+        held = lax.rem(owner[s], 2) == c
+        tile = p1d[owner[s] // 2]
+        top, bottom, dv = tile[0:32], tile[32:64], tile[64:96]
+        dc[s * 64 : s * 64 + 32, 0:128] = jnp.where(held, top, zero)
+        dc[s * 64 + 32 : s * 64 + 64, 0:128] = jnp.where(held, bottom, zero)
+        dc[s * 64 : s * 64 + 32, 128:256] = jnp.where(jnp.logical_and(held, lane < 64), dv, zero)
+        dc[s * 64 + 32 : s * 64 + 64, 128:256] = jnp.where(jnp.logical_and(held, lane >= 64), dv, zero)
+    hc_copy.wait_recv()
+
+    def packed(a):
+        v = a[:, 128:256]
+        v = v + pltpu.roll(v, 64, 1)
+        return a[:, 0:128], jnp.where(lane[0:16] < 64, v[0:16], v[16:32])
+
+    part_qk, part_v = packed(jnp.dot(hc[1], dc[...], preferred_element_type=F32))
+    swap[0, 0:32, :] = part_qk.astype(BF16)
+    swap[0, 32:48, :] = part_v.astype(BF16)
+    send(swap.at[0], swap.at[1], fwd_ss.at[3], fwd_rs.at[3], other)
+    swap_copy = sends[-1]
+    part_qk, part_v = packed(jnp.dot(hc[0], dc[...], preferred_element_type=F32))
 
     same = pl.ds(pl.multiple_of(c * 8, 8), 8)
-    for j, slot in reversed(list(enumerate(slots))):
-        arrived(p1d.at[slot], p1d_rs.at[slot])
-        send(p1d.at[slot], p1d.at[slot], p1d_ss.at[8 + j], p1d_rs.at[slot], other)
-    for slot in slots:
-        arrived(p1u.at[slot], p1u_rs.at[slot])
+    arrived(p1u.at[pl.ds(0, 7)], p1u_s.at[1])
     send(p1u.at[same], p1u.at[same], fwd_ss.at[0], fwd_rs.at[0], other)
     u_copy = sends[-1]
 
-    for copy in scalars:
-        copy.wait()
-
-    for i in range(8):
-        slot = (1 - c) * 8 + i
-        arrived(p1d.at[slot], p1d_rs.at[slot])
-
     def slot_of(s):
         return lax.rem(owner[s], 2) * 8 + owner[s] // 2
 
-    zero = jnp.zeros((32, 128), BF16)
-    for s in range(R):
-        of = slot_of(s)
-        dc[s * 64 : s * 64 + 64, 0:128] = p1d[of, 0:64, :]
-        dv = p1d[of, 64:96, :]
-        dc[s * 64 : s * 64 + 32, 128:256] = jnp.where(lane < 64, dv, zero)
-        dc[s * 64 + 32 : s * 64 + 64, 128:256] = jnp.where(lane < 64, zero, dv)
-    part_a = jnp.dot(hc[...], dc[...], preferred_element_type=F32)
-    part_v = part_a[:, 128:256]
-    part_v = part_v + pltpu.roll(part_v, 64, 1)
-    part_qk = part_a[:, 0:128].astype(BF16)
-    part_v = jnp.where(lane[0:16] < 64, part_v[0:16], part_v[16:32]).astype(BF16)
+    swap_copy.wait_recv()
+    part_qk = (part_qk + swap[1, 0:32, :].astype(F32)).astype(BF16)
+    part_v = (part_v + swap[1, 32:48, :].astype(F32)).astype(BF16)
     u_copy.wait_recv()
     for j, to in enumerate(heads):
         p2s[j, 0:32, :] = part_qk
@@ -204,24 +214,22 @@
         p2s[j, 48:80, :] = p1u[slot_of(2 * to)]
         p2s[j, 80:112, :] = p1u[slot_of(2 * to + 1)]
         if j < 7:
-            send(p2s.at[j], p2r.at[t], p2_ss.at[j], p2_rs.at[t], cross[j])
+            send(p2s.at[j], p2r.at[t], p2_s.at[0], p2_s.at[1], cross[j], late=True)
         else:
             p2r[t] = p2s[j]
 
-    for slot in slots:
-        arrived(p1o.at[slot], p1o_rs.at[slot])
+    arrived(p1o.at[pl.ds(0, 7)], p1o_s.at[1])
     send(p1o.at[same], p1o.at[same], fwd_ss.at[1], fwd_rs.at[1], other)
     sends[-1].wait_recv()
     for j, to in enumerate(heads):
         p2os[j, 0:48, :] = p1o[slot_of(2 * to)]
         p2os[j, 48:96, :] = p1o[slot_of(2 * to + 1)]
         if j < 7:
-            send(p2os.at[j], p2or.at[t], p2o_ss.at[j], p2o_rs.at[t], cross[j])
+            send(p2os.at[j], p2or.at[t], p2o_s.at[0], p2o_s.at[1], cross[j], late=True)
         else:
             p2or[t] = p2os[j]
 
-    for m in reversed(heads[:-1]):
-        arrived(p2r.at[m], p2_rs.at[m])
+    arrived(p2r.at[pl.ds(0, 7)], p2_s.at[1])
     a_qk = jnp.zeros((32, 128), F32)
     a_v = jnp.zeros((16, 128), F32)
     for m in range(T):
@@ -248,75 +256,94 @@
     for s in range(4):
         for h in range(4):
             q_s[(s * 4 + h) * 8 : (s * 4 + h) * 8 + 8, :] = q[s * 8 : s * 8 + 8, h * 128 : h * 128 + 128]
-    kn_s[0:32, :] = acc_kv[:, 0:128] + SCALE * d_qk[:, 512:640]
-    vn_s[0:32, :] = acc_kv[:, 128:256] + SCALE * d_val
-
-    for copy in cache:
-        copy.wait()
-    where = lax.broadcasted_iota(jnp.int32, (16, 1152), 1)
-    step = lax.broadcasted_iota(jnp.int32, (16, 1152), 0) // 4
-    fresh = jnp.logical_and(where >= 1024, where - 1024 <= step)
+    new_keys = (acc_kv[:, 0:128] + SCALE * d_qk[:, 512:640]).astype(BF16)
+    new_values = (acc_kv[:, 128:256] + SCALE * d_val).astype(BF16)
+    for pair in range(4):
+        for j in range(2):
+            k_v[pair, 1024:1056, j * 128 : j * 128 + 128] = new_keys
+            v_v[pair, 1024:1056, j * 128 : j * 128 + 128] = new_values
+
+    arrived(k_v.at[:, pl.ds(0, 1024), :], cache_sem.at[0])
+    arrived(v_v.at[:, pl.ds(0, 1024), :], cache_sem.at[1])
+    where = lax.broadcasted_iota(jnp.int32, (32, 1152), 1)
+    row = lax.broadcasted_iota(jnp.int32, (32, 1152), 0)
+    fresh = where - 1024
+    known = jnp.logical_and(fresh >= 0, fresh // 8 <= lax.rem(row, 16) // 4)
     factor = math.log2(math.e) / math.sqrt(HEAD_DIM)
-    for b in range(8):
-        k_v[b, 1024:1040, :] = kn_s[pl.ds(b, 16, stride=8), :].astype(BF16)
-        v_v[b, 1024:1040, :] = vn_s[pl.ds(b, 16, stride=8), :].astype(BF16)
-    for b in range(8):
-        qb = q_s[pl.ds(b, 16, stride=8), :].astype(BF16)
-        scores = lax.dot_general(qb, k_v[b], (((1,), (1,)), ((), ())), preferred_element_type=F32)
-        seen = jnp.logical_or(where < lengths[b], fresh)
+    blank = jnp.zeros((16, 128), BF16)
+    for pair in range(4):
+        b = 2 * pair
+        q0 = q_s[pl.ds(b, 16, stride=8), :].astype(BF16)
+        q1 = q_s[pl.ds(b + 1, 16, stride=8), :].astype(BF16)
+        both = jnp.concatenate(
+            [jnp.concatenate([q0, blank], axis=1), jnp.concatenate([blank, q1], axis=1)], axis=0
+        )
+        scores = lax.dot_general(both, k_v[pair], (((1,), (1,)), ((), ())), preferred_element_type=F32)
+        live = jnp.where(row < 16, lengths[b], lengths[b + 1])
+        seen = jnp.logical_or(
+            where < live, jnp.logical_and(known, lax.rem(fresh, 8) == b + row // 16)
+        )
         scores = jnp.where(seen, scores, MASKED)
         top = jnp.max(scores, axis=-1, keepdims=True)
         weights = jnp.exp2((scores - top) * factor)
         total = jnp.sum(weights, axis=-1, keepdims=True)
-        got = jnp.dot(weights.astype(BF16), v_v[b], preferred_element_type=F32)
-        ctx_s[pl.ds(b, 16, stride=8), :] = got / total
+        got = jnp.dot(weights.astype(BF16), v_v[pair], preferred_element_type=F32) / total
+        ctx_s[pl.ds(b, 16, stride=8), :] = got[0:16, 0:128]
+        ctx_s[pl.ds(b + 1, 16, stride=8), :] = got[16:32, 128:256]
     for s in range(4):
         for h in range(4):
             cx[s * 8 : s * 8 + 8, h * 128 : h * 128 + 128] = ctx_s[(s * 4 + h) * 8 : (s * 4 + h) * 8 + 8, :]
     context = cx[...].astype(BF16)
 
-    for m in reversed(heads[:-1]):
-        arrived(p2or.at[m], p2o_rs.at[m])
-    for m in range(T):
-        g, block = (m % 2) * 32, m // 2
-        for j in range(2):
-            tile = p2or[m, j * 48 : j * 48 + 32, :]
-            at = j * 512 + block * 128
-            uo_v[g : g + 32, at : at + 128] = tile
-            uo_v[64 + g : 96 + g, at : at + 128] = tile
-            do_v[m * 16 : m * 16 + 16, j * 128 : j * 128 + 128] = p2or[m, j * 48 + 32 : j * 48 + 48, :]
-    halves = jnp.concatenate(
-        [
-            jnp.concatenate([context[:, 0:128], context[:, 128:256]], axis=0),
-            jnp.concatenate([context[:, 256:384], context[:, 384:512]], axis=0),
-        ],
-        axis=1,
-    )
-    z_all = lax.dot_general(halves, do_v[...], (((1,), (1,)), ((), ())), preferred_element_type=F32)
-    z = jnp.where(lane < 64, z_all[0:32], z_all[32:64])
-    zs[...] = z.astype(BF16)
-    for j, peer in enumerate(cross):
-        send(zs, zr.at[t], z_ss.at[j], z_rs.at[t], peer)
+    def adapter_sums():
+        arrived(p2or.at[pl.ds(0, 7)], p2o_s.at[1])
+        for m in range(T):
+            g, block = (m % 2) * 32, m // 2
+            for j in range(2):
+                tile = p2or[m, j * 48 : j * 48 + 32, :]
+                at = j * 512 + block * 128
+                uo_v[g : g + 32, at : at + 128] = tile
+                uo_v[64 + g : 96 + g, at : at + 128] = tile
+                do_v[m * 16 : m * 16 + 16, j * 128 : j * 128 + 128] = p2or[m, j * 48 + 32 : j * 48 + 48, :]
+        halves = jnp.concatenate(
+            [
+                jnp.concatenate([context[:, 0:128], context[:, 128:256]], axis=0),
+                jnp.concatenate([context[:, 256:384], context[:, 384:512]], axis=0),
+            ],
+            axis=1,
+        )
+        z_all = lax.dot_general(halves, do_v[...], (((1,), (1,)), ((), ())), preferred_element_type=F32)
+        z = jnp.where(lane < 64, z_all[0:32], z_all[32:64])
+        zs[...] = z.astype(BF16)
+        for j, peer in enumerate(cross):
+            send(zs, zr.at[t], z_s.at[0], z_s.at[1], peer, late=True)
+        return z
 
     own = None
+    z = None
     for i in range(T):
         wo_copies[i].wait()
         part = jnp.dot(context, wo_v[i], preferred_element_type=F32)
         if i < T - 1:
             rss[i] = part.astype(BF16)
-            send(rss.at[i], rsr.at[t], rs_ss.at[i], rs_rs.at[t], cross[i])
+            send(rss.at[i], rsr.at[t], rs_ss.at[0], rs_rs.at[t], cross[i], late=True)
+            if i == 3:
+                z = adapter_sums()
         else:
             own = part
-    for m in reversed(heads[:-1]):
-        arrived(zr.at[m], z_rs.at[m])
+    for copy in sends:
+        copy.wait_send()
+    for ref, sem in ((p1d, p1d_s), (p1u, p1u_s), (p1o, p1o_s), (p2s, p2_s), (p2os, p2o_s), (zr, z_s)):
+        arrived(ref.at[pl.ds(0, 7)], sem.at[0])
+    arrived(zr.at[pl.ds(0, 7)], z_s.at[1])
+    for m in heads[:-1]:
         z = z + zr[m].astype(F32)
     own = own + SCALE * jnp.dot(z.astype(BF16), uo_v[...], preferred_element_type=F32)
     for m in reversed(heads[:-1]):
         arrived(rsr.at[m], rs_rs.at[m])
         own = own + rsr[m].astype(F32)
     out_ref[...] = own.astype(BF16)
-    for copy in sends:
-        copy.wait_send()
+    arrived(rss.at[pl.ds(0, 7)], rs_ss.at[0])
 
 
 def body(
@@ -337,8 +364,8 @@
             pltpu.VMEM((8192, 512), BF16),
             pltpu.VMEM((8192, 256), BF16),
             pltpu.VMEM((8, 512, 1024), BF16),
-            pltpu.VMEM((8, 1152, 128), BF16),
-            pltpu.VMEM((8, 1152, 128), BF16),
+            pltpu.VMEM((4, 1152, 256), BF16),
+            pltpu.VMEM((4, 1152, 256), BF16),
             pltpu.VMEM((3, 64, 128), BF16),
             pltpu.VMEM((2, 128, 128), BF16),
             pltpu.VMEM((64, 256), BF16),
@@ -347,10 +374,11 @@
             pltpu.VMEM((64, 512), BF16),
             pltpu.VMEM((4, 64, 128), BF16),
             pltpu.VMEM((128, 128), BF16),
-            pltpu.VMEM((16, 96, 128), BF16),
+            pltpu.VMEM((8, 96, 128), BF16),
             pltpu.VMEM((16, 32, 128), BF16),
             pltpu.VMEM((16, 48, 128), BF16),
-            pltpu.VMEM((32, 1024), BF16),
+            pltpu.VMEM((2, 32, 1024), BF16),
+            pltpu.VMEM((2, 48, 128), BF16),
             pltpu.VMEM((1024, 256), BF16),
             pltpu.VMEM((8, 112, 128), BF16),
             pltpu.VMEM((8, 112, 128), BF16),
@@ -358,8 +386,6 @@
             pltpu.VMEM((8, 96, 128), BF16),
             pltpu.VMEM((128, 640), BF16),
             pltpu.VMEM((128, 128), BF16),
-            pltpu.VMEM((128, 128), F32),
-            pltpu.VMEM((128, 128), F32),
             pltpu.VMEM((128, 128), F32),
             pltpu.VMEM((32, 512), F32),
             pltpu.VMEM((32, 256), F32),
@@ -374,8 +400,7 @@
             pltpu.SMEM((R,), jnp.int32),
             pltpu.SMEM((8,), jnp.int32),
             dma((8,)), dma((K_PARTS,)), dma((2, K_PARTS)), dma((2,)), dma((T,)),
-            dma((15,)), dma((R,)), dma((7,)), dma((R,)), dma((7,)), dma((R,)), dma((2,)), dma((2,)),
-            dma((7,)), dma((T,)), dma((7,)), dma((T,)), dma((7,)), dma((T,)), dma((7,)), dma((T,)),
+            dma((2,)), dma((2,)), dma((2,)), dma((4,)), dma((4,)), dma((2,)), dma((2,)), dma((1,)), dma((T,)), dma((2,)),
         ],
         compiler_params=pltpu.CompilerParams(
             collective_id=0, has_side_effects=True, vmem_limit_bytes=60 * 1024 * 1024

time: 35.8 us -> 33.3 us (0.930)
  Pallas kernels: 35.1 us -> 32.6 us
    pallas_call x1, Pallas kernels: 35.1 us -> 32.6 us  [body(): pl.pallas_call(kernel, out_shape=pltpu.VMEM((rows, 1024), BF16), in_specs...]
where the time goes in v3:
time: 33.3 us; the launch traced here: 33.2 us
  Pallas kernels  32.6 us (98%)
  local copies, waits for them, and re-layouts  0.63 us (2%)
    pallas_call x1, Pallas kernels, body(): pl.pallas_call(kernel, out_shape=pltpu.VMEM((rows, 1024), BF16), in_specs...  32.6 us

profile of v3, /device:TPU:1, one launch (start us, length us, event | category | flops | bytes accessed | tf_op | source)
XLA Modules:
  0.0 33.2 jit_solution(17496924289324737643)
XLA Ops:
  0.0 32.6 %adapter_attention.1 = bf16[32,1024]{1,0:T(8,128)(2,1)S(1)} custom-call(s32[16]{0:T(128)} %owner_any.1, s32[8]{0:T(128)} %lengths_any.1, bf16[32,8192]{1,0:T(8,128)(2,1)} %bitcast.5, bf16[8192,512]{1,0:T(8,128)(2,1)} %wq.1, bf16[2,8192,128]{2,1,0:T(8,128)(2,1)} %wkv.1, bf16[512,8192]{1,0:T(8,128)(2,1)} %wo.1, bf16[3,64,512]{2,1,0:T(8,128)(2,1)} %bitcast.6, ...), custom_call_target="tpu_custom_call" | custom-call | tf_op jit(solution)/shard_map/adapter_attention/pallas_call | solution.py:357
  32.6 0.6 %copy.15 = bf16[4,8,1024]{2,1,0:T(8,128)(2,1)} copy(bf16[4,8,1024]{2,1,0:T(8,128)(2,1)S(1)} %bitcast.4) | data formatting | bytes 131072

commit v4 on v3

--- a/solution.py
+++ b/solution.py
@@ -37,10 +37,10 @@
         (lax.rem(x + dx, 4) * 4 + (zl if dz == 0 else 1 - zl) * 2 + c, t)
         for dx, dz in ((2, 1), (1, 1), (3, 1), (2, 0), (1, 0), (3, 0), (0, 1))
     ]
-    heads = [
-        (zh if dz == 0 else 1 - zh) * 4 + lax.rem(y + dy, 4)
-        for dz, dy in ((1, 2), (1, 1), (1, 3), (0, 2), (1, 0), (0, 1), (0, 3), (0, 0))
-    ]
+    heads = []
+    for first, second in zip([(1, 2), (1, 1), (1, 3), (0, 2), (1, 0), (0, 1), (0, 3), (0, 0)], [(0, 2), (1, 1), (1, 2), (1, 3), (0, 1), (1, 0), (0, 3), (0, 0)]):
+        dz, dy = first[0] * (1 - c) + second[0] * c, first[1] * (1 - c) + second[1] * c
+        heads.append(lax.rem(zh + dz, 2) * 4 + lax.rem(y + dy, 4))
     cross = [(r, to) for to in heads[:-1]]
 
     barrier = pltpu.get_barrier_semaphore()
@@ -135,7 +135,7 @@
         copy.start()
     wo_copies = [
         pltpu.make_async_copy(
-            wo.at[:, pl.ds(pl.multiple_of(heads[i] * 1024, 1024), 1024)], wo_v.at[i], wo_sem.at[i]
+            wo.at[:, pl.ds(pl.multiple_of(heads[i] * 1024, 1024), 1024)], wo_v.at[i], wo_sem.at[0]
         )
         for i in range(T)
     ]
@@ -319,10 +319,11 @@
             send(zs, zr.at[t], z_s.at[0], z_s.at[1], peer, late=True)
         return z
 
+    arrived(wo_v, wo_sem.at[0])
+
     own = None
     z = None
     for i in range(T):
-        wo_copies[i].wait()
         part = jnp.dot(context, wo_v[i], preferred_element_type=F32)
         if i < T - 1:
             rss[i] = part.astype(BF16)
@@ -399,7 +400,7 @@
             pltpu.VMEM((8, 32, 128), BF16),
             pltpu.SMEM((R,), jnp.int32),
             pltpu.SMEM((8,), jnp.int32),
-            dma((8,)), dma((K_PARTS,)), dma((2, K_PARTS)), dma((2,)), dma((T,)),
+            dma((8,)), dma((K_PARTS,)), dma((2, K_PARTS)), dma((2,)), dma((1,)),
             dma((2,)), dma((2,)), dma((2,)), dma((4,)), dma((4,)), dma((2,)), dma((2,)), dma((1,)), dma((T,)), dma((2,)),
         ],
         compiler_params=pltpu.CompilerParams(

time: 33.3 us -> 33.2 us (level)
  no operation moved by 1% of the time
where the time goes in v4:
time: 33.2 us; the launch traced here: 33.1 us
  Pallas kernels  32.4 us (98%)
  local copies, waits for them, and re-layouts  0.63 us (2%)
    pallas_call x1, Pallas kernels, body(): pl.pallas_call(kernel, out_shape=pltpu.VMEM((rows, 1024), BF16), in_specs...  32.4 us

profile of v4, /device:TPU:1, one launch (start us, length us, event | category | flops | bytes accessed | tf_op | source)
XLA Modules:
  0.0 33.1 jit_solution(563383887556767997)
XLA Ops:
  0.0 32.4 %adapter_attention.1 = bf16[32,1024]{1,0:T(8,128)(2,1)S(1)} custom-call(s32[16]{0:T(128)} %owner_any.1, s32[8]{0:T(128)} %lengths_any.1, bf16[32,8192]{1,0:T(8,128)(2,1)} %bitcast.5, bf16[8192,512]{1,0:T(8,128)(2,1)} %wq.1, bf16[2,8192,128]{2,1,0:T(8,128)(2,1)} %wkv.1, bf16[512,8192]{1,0:T(8,128)(2,1)} %wo.1, bf16[3,64,512]{2,1,0:T(8,128)(2,1)} %bitcast.6, ...), custom_call_target="tpu_custom_call" | custom-call | tf_op jit(solution)/shard_map/adapter_attention/pallas_call | solution.py:358
  32.4 0.6 %copy.15 = bf16[4,8,1024]{2,1,0:T(8,128)(2,1)} copy(bf16[4,8,1024]{2,1,0:T(8,128)(2,1)S(1)} %bitcast.4) | data formatting | bytes 131072
